TPU v7x, 256 devices: a whole 4x4x8 slice. The times are simulated.
256 devices in a mesh: dp: 8 (over x, y_lo), expert: 32 (over y_hi, z, core).
Axes of the slice: x: 4, y: 4 (y_hi: 2, y_lo: 2; y = y_hi * 2 + y_lo), z: 8, core: 2. Of those that a mesh axis runs over, the one named last changes fastest.
Arguments:
- tokens: bfloat16 [2, 16384, 2048], P(None, ('dp', 'expert')), may hold values from -6 to 6
- route_ids: int32 [2, 16384, 10], P(None, ('dp', 'expert')), may hold values from 0 to 63, all different within a row; in each aligned block of 64 rows (0 to 63, 64 to 127, ..., all dimensions but the last counted through in order) at most 12 rows name the same one
- route_gates: float32 [2, 16384, 10], P(None, ('dp', 'expert')), may hold values from 0.1 to 1
- expert_in: bfloat16 [32, 2, 2048, 1024], P('expert', None, 'dp'), may hold values from -0.125 to 0.125
- expert_out: bfloat16 [32, 2, 512, 2048], P('expert', None, None, 'dp'), may hold values from -0.25 to 0.25
- old_plan: int32 [32], replicated, may hold values from 0 to 31, each once
- new_plan: int32 [32], replicated, may hold values from 0 to 31, each once
Outputs:
- mixed: bfloat16 [2, 16384, 2048], P(None, ('dp', 'expert'))
- moved_in: bfloat16 [32, 2048, 1024], P('expert', 'dp')
- moved_out: bfloat16 [32, 512, 2048], P('expert', None, 'dp')
Inputs may be any that keep to these rules, and one draw needn't show every extreme that they name: `route_ids`: each token names 10 different experts. In each micro-batch the 64 tokens of one device name no expert in more than 12 of their routes, and some expert in exactly 12. `old_plan`: each movable expert is held by exactly one slot. `new_plan`: each movable expert is held by exactly one slot.
All inputs are finite; a program needn't handle non-finite values.
Results may differ from a plain program's by a relative error of at most 0.0057.
Values may be sent and summed in bfloat16 or wider, within the bound.
A program may use at most 128 MiB of HBM per device.

v0:
```python
import jax
import jax.numpy as jnp
from jax import lax
from jax.sharding import PartitionSpec as P


def inverse(assignment):
    count = assignment.shape[0]
    return jnp.zeros((count,), jnp.int32).at[assignment].set(jnp.arange(count, dtype=jnp.int32))


def slot_rank(slots, slot_count):
    row_count = slots.shape[0]
    block_rows = 128
    padded_rows = -(-row_count // block_rows) * block_rows
    onehot = (slots[:, None] == jnp.arange(slot_count, dtype=jnp.int32)[None, :]).astype(
        jnp.float32
    )
    shaped = onehot.reshape(padded_rows // block_rows, block_rows, slot_count)
    positions = jnp.arange(block_rows, dtype=jnp.int32)
    triangle = (positions[:, None] > positions[None, :]).astype(jnp.float32)
    inside = jnp.einsum("ij,bjs->bis", triangle, shaped, precision=lax.Precision.HIGHEST)
    block_totals = jnp.sum(shaped, axis=1)
    preceding = jnp.cumsum(block_totals, axis=0) - block_totals
    counted = jnp.sum((inside + preceding[:, None, :]) * shaped, axis=2)
    return counted.reshape(-1).astype(jnp.int32)


def slot_targets(chosen, assignment, capacity):
    groups = assignment.shape[0]
    placed = inverse(assignment)
    movable = chosen >= groups
    offset = jnp.clip(chosen - groups, 0, groups - 1)
    slots = jnp.where(movable, placed[offset] * 2 + 1, chosen * 2).reshape(-1)
    before = slot_rank(slots, 2 * groups)
    return slots * capacity + before


def expert_apply(picked, weight_in, weight_out):
    hidden_units = weight_out.shape[0]
    projected = jnp.dot(picked, weight_in, preferred_element_type=jnp.float32)
    hidden = (jax.nn.silu(projected[:, :hidden_units]) * projected[:, hidden_units:]).astype(
        jnp.bfloat16
    )
    return jnp.dot(hidden, weight_out, preferred_element_type=jnp.float32).astype(jnp.bfloat16)


def micro_batch(batch_tokens, chosen, gates, assignment, weight_pairs, capacity):
    tok_count, width = batch_tokens.shape
    topk = chosen.shape[1]
    groups = assignment.shape[0]
    target = slot_targets(chosen, assignment, capacity)
    sources = jnp.repeat(batch_tokens, topk, axis=0)
    outgoing = jnp.zeros((2 * groups * capacity, width), jnp.bfloat16).at[target].set(sources)
    arrived = lax.all_to_all(
        outgoing.reshape(groups, 2, capacity, width),
        "expert",
        split_axis=0,
        concat_axis=0,
        tiled=True,
    )
    results = []
    for slot_index in range(2):
        picked = arrived[:, slot_index].reshape(groups * capacity, width)
        result = expert_apply(picked, weight_pairs[slot_index][0], weight_pairs[slot_index][1])
        results.append(result.reshape(groups, capacity, width))
    returned = lax.all_to_all(
        jnp.stack(results, axis=1), "expert", split_axis=0, concat_axis=0, tiled=True
    )
    fetched = returned.reshape(-1, width)[target].reshape(tok_count, topk, width)
    summed = jnp.sum(gates[:, :, None] * fetched.astype(jnp.float32), axis=1)
    return summed.astype(jnp.bfloat16)


def relocate(expert_in, expert_out, old_plan, new_plan):
    pieces_in, pieces_out = (
        lax.all_to_all(expert_in[:, 1], "expert", split_axis=1, concat_axis=0, tiled=True),
        lax.all_to_all(expert_out[:, 1], "expert", split_axis=1, concat_axis=0, tiled=True),
    )
    source = inverse(old_plan)[new_plan]
    return (
        lax.all_to_all(pieces_in[source], "expert", split_axis=0, concat_axis=1, tiled=True),
        lax.all_to_all(pieces_out[source], "expert", split_axis=0, concat_axis=1, tiled=True),
    )


def on_device(tokens, route_ids, route_gates, expert_in, expert_out, old_plan, new_plan):
    groups = lax.axis_size("expert")
    mb_count, tok_count, width = tokens.shape
    topk = route_ids.shape[2]
    capacity = min(tok_count, tok_count * topk * 5 // (8 * groups))
    outputs = []
    full_in, full_out = (
        lax.all_gather(expert_in, "dp", axis=2, tiled=True),
        lax.all_gather(expert_out, "dp", axis=3, tiled=True),
    )
    weight_pairs = [(full_in[0, 0], full_out[0, 0]), (full_in[0, 1], full_out[0, 1])]
    outputs.append(
        micro_batch(tokens[0], route_ids[0], route_gates[0], old_plan, weight_pairs, capacity)
    )
    moved_in, moved_out = relocate(expert_in, expert_out, old_plan, new_plan)
    mobile_in, mobile_out = (
        lax.all_gather(moved_in, "dp", axis=1, tiled=True),
        lax.all_gather(moved_out, "dp", axis=2, tiled=True),
    )
    weight_pairs = [weight_pairs[0], (mobile_in[0], mobile_out[0])]
    outputs.append(
        micro_batch(tokens[1], route_ids[1], route_gates[1], new_plan, weight_pairs, capacity)
    )
    return (jnp.stack(outputs), moved_in, moved_out)


def solution(mesh):
    in_specs = (
        P(None, ("dp", "expert"), None),
        P(None, ("dp", "expert"), None),
        P(None, ("dp", "expert"), None),
        P("expert", None, "dp", None),
        P("expert", None, None, "dp"),
        P(),
        P(),
    )
    out_specs = (P(None, ("dp", "expert"), None), P("expert", "dp", None), P("expert", None, "dp"))
    return jax.shard_map(
        on_device, mesh=mesh, in_specs=in_specs, out_specs=out_specs, check_vma=False
    )
```

profile of v0, /device:TPU:1, one launch (start us, length us, event | category | flops | bytes accessed | tf_op | source)
XLA Modules:
  0.0 711.5 jit_solution(862656621901775317)
XLA Ops:
  13.5 12.8 %all-to-all-start.5 = ((bf16[32,2,2048]{2,1,0:T(2,128)(2,1)}), bf16[32,2,2048]{2,1,0:T(2,128)(2,1)S(1)}, u32[]{:S(2)}, u32[]{:S(2)}) async-start(bf16[32,2,2048]{2,1,0:T(2,128)(2,1)} %reshape.485), calls=%async_computation.5 | async-start | bytes 524288 | tf_op jit(solution)/shard_map/all_to_all | solution.py:78
  32.1 11.8 %all-to-all-done.5 = bf16[32,2,2048]{2,1,0:T(2,128)(2,1)S(1)} async-done(((bf16[32,2,2048]{2,1,0:T(2,128)(2,1)}), bf16[32,2,2048]{2,1,0:T(2,128)(2,1)S(1)}, u32[]{:S(2)}, u32[]{:S(2)}) %all-to-all-start.5) | async-done | bytes 262176 | tf_op jit(solution)/shard_map/all_to_all | solution.py:78
  43.9 7.5 %all-to-all-start.3 = ((bf16[32,2,4096]{2,1,0:T(2,128)(2,1)}), bf16[32,2,4096]{2,1,0:T(2,128)(2,1)S(1)}, u32[]{:S(2)}, u32[]{:S(2)}) async-start(bf16[32,2,4096]{2,1,0:T(2,128)(2,1)} %reshape.487), calls=%async_computation.3 | async-start | bytes 1048576 | tf_op jit(solution)/shard_map/all_to_all | solution.py:77
  54.4 15.0 %all-to-all-done.3 = bf16[32,2,4096]{2,1,0:T(2,128)(2,1)S(1)} async-done(((bf16[32,2,4096]{2,1,0:T(2,128)(2,1)}), bf16[32,2,4096]{2,1,0:T(2,128)(2,1)S(1)}, u32[]{:S(2)}, u32[]{:S(2)}) %all-to-all-start.3) | async-done | bytes 524320 | tf_op jit(solution)/shard_map/all_to_all | solution.py:77
  69.4 5.8 all-to-all-start.6
  82.7 6.2 all-to-all-done.6
  88.9 5.9 all-to-all-start.4
  98.1 5.5 reshape.433
  103.9 8.8 %scatter_custom_fusion.1 = bf16[768,2048]{1,0:T(8,128)(2,1)S(1)} fusion(s32[640]{0:T(1024)S(1)} %fusion.37, bf16[640,2048]{1,0:T(8,128)(2,1)} %reshape.433, bf16[]{:T(256)} %constant.11.clone.1), kind=kCustom, calls=%fused_computation.35 | custom fusion | bytes 3146240 | tf_op jit(solution)/shard_map/scatter | solution.py:54
  115.4 7.1 copy.80
  122.5 9.9 %all-to-all-start = ((bf16[32,2,12,2048]{3,1,2,0:T(2,128)(2,1)}), bf16[32,2,12,2048]{3,1,2,0:T(2,128)(2,1)S(1)}, u32[]{:S(2)}, u32[]{:S(2)}) async-start(bf16[32,2,12,2048]{3,1,2,0:T(2,128)(2,1)} %copy.80), calls=%async_computation | async-start | bytes 6291456 | tf_op jit(solution)/shard_map/all_to_all | solution.py:55
  141.4 5.5 reshape.449
  147.2 9.9 %scatter_custom_fusion.3 = bf16[768,2048]{1,0:T(8,128)(2,1)} fusion(s32[640]{0:T(1024)S(1)} %fusion.38, bf16[640,2048]{1,0:T(8,128)(2,1)} %reshape.449, bf16[]{:T(256)} %constant.11.clone.1), kind=kCustom, calls=%fused_computation.33 | custom fusion | bytes 3146240 | tf_op jit(solution)/shard_map/scatter | solution.py:54
  157.1 6.1 reshape.361
  163.2 7.2 %copy.91 = bf16[32,2,12,2048]{3,1,2,0:T(2,128)(2,1)} copy(bf16[32,2,12,2048]{3,2,1,0:T(8,128)(2,1)} %reshape.361) | data formatting | bytes 6291456 | tf_op jit(solution)/shard_map/reshape | solution.py:56
  170.3 35.7 %all-to-all-done = bf16[32,2,12,2048]{3,1,2,0:T(2,128)(2,1)S(1)} async-done(((bf16[32,2,12,2048]{3,1,2,0:T(2,128)(2,1)}), bf16[32,2,12,2048]{3,1,2,0:T(2,128)(2,1)S(1)}, u32[]{:S(2)}, u32[]{:S(2)}) %all-to-all-start) | async-done | bytes 3145760 | tf_op jit(solution)/shard_map/all_to_all | solution.py:55
  206.0 9.6 %all-to-all-start.2 = ((bf16[32,2,12,2048]{3,1,2,0:T(2,128)(2,1)}), bf16[32,2,12,2048]{3,1,2,0:T(2,128)(2,1)}, u32[]{:S(2)}, u32[]{:S(2)}) async-start(bf16[32,2,12,2048]{3,1,2,0:T(2,128)(2,1)} %copy.91), calls=%async_computation.2 | async-start | bytes 6291456 | tf_op jit(solution)/shard_map/all_to_all | solution.py:55
  215.7 18.1 %slice_reduce_fusion.3 = (bf16[32,12,2048]{2,1,0:T(8,128)(2,1)}, bf16[32,12,2048]{2,1,0:T(8,128)(2,1)}) fusion(bf16[32,2,12,2048]{3,1,2,0:T(2,128)(2,1)S(1)} %all-to-all-done), kind=kLoop, calls=%fused_computation.25 | loop fusion | bytes 6291456 | tf_op jit(solution)/shard_map/slice | solution.py:64
  238.9 13.2 %all-gather.5.cloned.1.call-done = bf16[1,2,2048,1024]{3,2,1,0:T(8,128)(2,1)} async-done(((bf16[1,2,256,1024]{3,2,1,0:T(8,128)(2,1)}), bf16[1,2,2048,1024]{3,2,1,0:T(8,128)(2,1)}) %all-gather.5.cloned.1.call-update) | async-done | bytes 8388624 | tf_op jit(solution)/shard_map/all_gather | solution.py:94
  256.6 110.5 %all-gather.7.cloned.1.call-done = bf16[1,2,512,2048]{3,2,1,0:T(8,128)(2,1)} async-done(((bf16[1,2,512,256]{3,2,1,0:T(8,128)(2,1)}), bf16[1,2,512,2048]{3,2,1,0:T(8,128)(2,1)}) %all-gather.7.cloned.1.call-update) | async-done | bytes 4194320 | tf_op jit(solution)/shard_map/all_gather | solution.py:95
  390.6 10.2 %all-to-all-start.1 = ((bf16[32,2,12,2048]{3,1,2,0:T(2,128)(2,1)}), bf16[32,2,12,2048]{3,1,2,0:T(2,128)(2,1)S(1)}, u32[]{:S(2)}, u32[]{:S(2)}) async-start(bf16[32,2,12,2048]{3,1,2,0:T(2,128)(2,1)} %copy.81), calls=%async_computation.1 | async-start | bytes 6291456 | tf_op jit(solution)/shard_map/all_to_all | solution.py:67
  401.4 17.5 %slice_reduce_fusion.1 = (bf16[32,12,2048]{2,1,0:T(8,128)(2,1)}, bf16[32,12,2048]{2,1,0:T(8,128)(2,1)}) fusion(bf16[32,2,12,2048]{3,1,2,0:T(2,128)(2,1)} %all-to-all-done.2), kind=kLoop, calls=%fused_computation.23 | loop fusion | bytes 6291456 | tf_op jit(solution)/shard_map/slice | solution.py:64
  426.1 70.8 %all-gather.9.cloned.1.call-done = bf16[1,2048,1024]{2,1,0:T(8,128)(2,1)} async-done(((bf16[1,256,1024]{2,1,0:T(8,128)(2,1)}), bf16[1,2048,1024]{2,1,0:T(8,128)(2,1)}) %all-gather.9.cloned.1.call-update) | async-done | bytes 4194320 | tf_op jit(solution)/shard_map/all_gather | solution.py:103
  496.9 5.6 fusion.1
  502.5 58.6 %all-gather.11.cloned.1.call-done = bf16[1,512,2048]{2,1,0:T(8,128)(2,1)} async-done(((bf16[1,512,256]{2,1,0:T(8,128)(2,1)}), bf16[1,512,2048]{2,1,0:T(8,128)(2,1)}) %all-gather.11.cloned.1.call-update) | async-done | bytes 2097168 | tf_op jit(solution)/shard_map/all_gather | solution.py:104
  582.3 5.0 copy.94
  587.3 11.5 %all-to-all-start.7 = ((bf16[32,2,12,2048]{3,1,2,0:T(2,128)(2,1)}), bf16[32,2,12,2048]{3,1,2,0:T(2,128)(2,1)}, u32[]{:S(2)}, u32[]{:S(2)}) async-start(bf16[32,2,12,2048]{3,1,2,0:T(2,128)(2,1)} %copy.94), calls=%async_computation.7 | async-start | bytes 6291456 | tf_op jit(solution)/shard_map/all_to_all | solution.py:67
  611.5 5.9 reshape.363
  617.4 55.1 %all-to-all-done.7 = bf16[32,2,12,2048]{3,1,2,0:T(2,128)(2,1)} async-done(((bf16[32,2,12,2048]{3,1,2,0:T(2,128)(2,1)}), bf16[32,2,12,2048]{3,1,2,0:T(2,128)(2,1)}, u32[]{:S(2)}, u32[]{:S(2)}) %all-to-all-start.7) | async-done | bytes 3145760 | tf_op jit(solution)/shard_map/all_to_all | solution.py:67
  672.5 5.5 copy.95
  686.8 5.9 reshape.364
  692.7 6.0 multiply_reduce_fusion.1
  (138 shorter events, 127.2 us)
Async XLA Ops:
  7.2 19.1 %copy-start.2 = (bf16[1,2,256,1024]{3,2,1,0:T(8,128)(2,1)S(1)}, bf16[1,2,256,1024]{3,2,1,0:T(8,128)(2,1)}, u32[]{:S(2)}) copy-start(bf16[1,2,256,1024]{3,2,1,0:T(8,128)(2,1)} %param.10) | copy-start | bytes 3145732
  7.2 244.9 %all-gather.5.cloned.1.call-start = ((), (), s32[]{:S(2)}) async-start(), calls=%async_computation.8 | async-start | bytes 9437184 | tf_op jit(solution)/shard_map/all_gather | solution.py:94
  7.9 359.1 %all-gather.7.cloned.1.call-start = ((), (), s32[]{:S(2)}) async-start(), calls=%async_computation.9 | async-start | bytes 4718592 | tf_op jit(solution)/shard_map/all_gather | solution.py:95
  13.5 30.3 %all-to-all-start.5 = ((bf16[32,2,2048]{2,1,0:T(2,128)(2,1)}), bf16[32,2,2048]{2,1,0:T(2,128)(2,1)S(1)}, u32[]{:S(2)}, u32[]{:S(2)}) async-start(bf16[32,2,2048]{2,1,0:T(2,128)(2,1)} %reshape.485), calls=%async_computation.5 | async-start | bytes 524288 | tf_op jit(solution)/shard_map/all_to_all | solution.py:78
  26.3 5.7 copy-start.11
  26.3 5.7 copy-start.12
  26.4 26.4 %copy-start.7 = (s32[2,64,10]{1,0,2:T(2,128)S(1)}, s32[2,64,10]{1,0,2:T(2,128)}, u32[]{:S(2)}) copy-start(s32[2,64,10]{1,0,2:T(2,128)} %param.8) | copy-start | bytes 15364
  43.9 25.6 %all-to-all-start.3 = ((bf16[32,2,4096]{2,1,0:T(2,128)(2,1)}), bf16[32,2,4096]{2,1,0:T(2,128)(2,1)S(1)}, u32[]{:S(2)}, u32[]{:S(2)}) async-start(bf16[32,2,4096]{2,1,0:T(2,128)(2,1)} %reshape.487), calls=%async_computation.3 | async-start | bytes 1048576 | tf_op jit(solution)/shard_map/all_to_all | solution.py:77
  69.4 19.5 %all-to-all-start.6 = ((bf16[32,16,256]{2,1,0:T(8,128)(2,1)}), bf16[32,16,256]{2,1,0:T(8,128)(2,1)S(1)}, u32[]{:S(2)}, u32[]{:S(2)}) async-start(bf16[32,16,256]{2,1,0:T(8,128)(2,1)} %gather_fusion.5), calls=%async_computation.6 | async-start | bytes 524288 | tf_op jit(solution)/shard_map/all_to_all | solution.py:83
  80.6 14.2 %copy-start.6 = (bf16[2,64,2048]{2,1,0:T(8,128)(2,1)S(1)}, bf16[2,64,2048]{2,1,0:T(8,128)(2,1)}, u32[]{:S(2)}) copy-start(bf16[2,64,2048]{2,1,0:T(8,128)(2,1)} %param.7) | copy-start | bytes 1572868
  88.9 9.2 %copy-start.3 = (bf16[32,16,256]{2,1,0:T(8,128)(2,1)}, bf16[32,16,256]{2,1,0:T(8,128)(2,1)S(1)}, u32[]{:S(2)}) copy-start(bf16[32,16,256]{2,1,0:T(8,128)(2,1)S(1)} %all-to-all-done.6) | copy-start | bytes 786436
  88.9 33.6 %all-to-all-start.4 = ((bf16[32,8,1024]{2,1,0:T(8,128)(2,1)}), bf16[32,8,1024]{2,1,0:T(8,128)(2,1)}, u32[]{:S(2)}, u32[]{:S(2)}) async-start(bf16[32,8,1024]{2,1,0:T(8,128)(2,1)} %gather_fusion.4), calls=%async_computation.4 | async-start | bytes 1048576 | tf_op jit(solution)/shard_map/all_to_all | solution.py:82
  122.5 83.5 %all-to-all-start = ((bf16[32,2,12,2048]{3,1,2,0:T(2,128)(2,1)}), bf16[32,2,12,2048]{3,1,2,0:T(2,128)(2,1)S(1)}, u32[]{:S(2)}, u32[]{:S(2)}) async-start(bf16[32,2,12,2048]{3,1,2,0:T(2,128)(2,1)} %copy.80), calls=%async_computation | async-start | bytes 6291456 | tf_op jit(solution)/shard_map/all_to_all | solution.py:55
  132.4 364.5 %all-gather.9.cloned.1.call-start = ((), (), s32[]{:S(2)}) async-start(), calls=%async_computation.10 | async-start | bytes 4718592 | tf_op jit(solution)/shard_map/all_gather | solution.py:103
  134.1 4.6 copy-start.5
  206.0 184.6 %all-to-all-start.2 = ((bf16[32,2,12,2048]{3,1,2,0:T(2,128)(2,1)}), bf16[32,2,12,2048]{3,1,2,0:T(2,128)(2,1)}, u32[]{:S(2)}, u32[]{:S(2)}) async-start(bf16[32,2,12,2048]{3,1,2,0:T(2,128)(2,1)} %copy.91), calls=%async_computation.2 | async-start | bytes 6291456 | tf_op jit(solution)/shard_map/all_to_all | solution.py:55
  233.8 3.8 copy-start.1
  373.2 4.6 copy-start.9
  390.6 196.7 %all-to-all-start.1 = ((bf16[32,2,12,2048]{3,1,2,0:T(2,128)(2,1)}), bf16[32,2,12,2048]{3,1,2,0:T(2,128)(2,1)S(1)}, u32[]{:S(2)}, u32[]{:S(2)}) async-start(bf16[32,2,12,2048]{3,1,2,0:T(2,128)(2,1)} %copy.81), calls=%async_computation.1 | async-start | bytes 6291456 | tf_op jit(solution)/shard_map/all_to_all | solution.py:67
  400.8 160.4 %all-gather.11.cloned.1.call-start = ((), (), s32[]{:S(2)}) async-start(), calls=%async_computation.11 | async-start | bytes 2359296 | tf_op jit(solution)/shard_map/all_gather | solution.py:104
  569.1 4.6 copy-start.10
  587.3 11.5 %copy-start.8 = (f32[2,64,10]{1,0,2:T(2,128)S(1)}, f32[2,64,10]{1,0,2:T(2,128)}, u32[]{:S(2)}) copy-start(f32[2,64,10]{1,0,2:T(2,128)} %param.9) | copy-start | bytes 15364
  587.3 85.2 %all-to-all-start.7 = ((bf16[32,2,12,2048]{3,1,2,0:T(2,128)(2,1)}), bf16[32,2,12,2048]{3,1,2,0:T(2,128)(2,1)}, u32[]{:S(2)}, u32[]{:S(2)}) async-start(bf16[32,2,12,2048]{3,1,2,0:T(2,128)(2,1)} %copy.94), calls=%async_computation.7 | async-start | bytes 6291456 | tf_op jit(solution)/shard_map/all_to_all | solution.py:67
  692.7 6.0 copy-start
  698.7 5.3 copy-start.4
Sparse Core Ops, SparseCore 0:
  9.8 242.2 all-gather.4
  253.8 113.1 all-gather.6
  368.8 128.0 all-gather.8
  499.0 62.0 all-gather.10
where the time goes:
time: 722 us; the launch traced here: 711 us
  waiting for transfers between devices  379 us (52%)
  local copies, waits for them, and re-layouts  192 us (27%)
  starting transfers between devices  73.3 us (10%)
  matrix products  32.1 us (4%)
  other arithmetic  20.7 us (3%)
  between operations  14.6 us (2%)
    all_gather x1, waiting for transfers between devices, on_device(): lax.all_gather(expert_out, 'dp', axis=3, tiled=True)  110 us
    all_gather x1, waiting for transfers between devices, on_device(): lax.all_gather(moved_in, 'dp', axis=1, tiled=True)  70.8 us
    all_gather x1, waiting for transfers between devices, on_device(): lax.all_gather(moved_out, 'dp', axis=2, tiled=True)  58.6 us
    all_to_all x2, waiting for transfers between devices, micro_batch(): lax.all_to_all(jnp.stack(results, axis=1), 'expert', split_axis=0, concat...  55.1 us
    all_to_all x2, waiting for transfers between devices, micro_batch(): lax.all_to_all(outgoing.reshape(groups, 2, capacity, width), 'expert', sp...  35.7 us
    slice x2, local copies, waits for them, and re-layouts, micro_batch(): picked = arrived[:, slot_index].reshape(groups * capacity, width)  35.6 us
    another operation x6, local copies, waits for them, and re-layouts, micro_batch(): jnp.stack(results, axis=1)  23.1 us
    reshape x4, local copies, waits for them, and re-layouts, micro_batch(): outgoing.reshape(groups, 2, capacity, width)  23 us
  transfers between devices with their start and end apart: 12, of which 9 were waited for; matrix products, arithmetic and copies ran while one was open for 30% of the time, Pallas kernels for 0%

commit v1 on v0

v1 whole, which is shorter than its diff:
```python
import jax
import jax.numpy as jnp
from jax import lax
from jax.experimental import pallas as pl
from jax.experimental.pallas import tpu as pltpu
from jax.sharding import PartitionSpec as P

MESH = pl.DeviceIdType.MESH
NX, NYL, NYH, NZ, NC = 4, 2, 2, 8, 2
NDP, NEX = NX * NYL, NYH * NZ * NC
MB, TOK, D, F, TOPK, CAP = 2, 64, 2048, 512, 10, 12
DK = D // NDP
GRP = NYH * NC * TOK
ROWS = NYH * NC * CAP
WIDE = D + 128
NB = 512
BF, F32 = jnp.bfloat16, jnp.float32


def kernel(
    tokens, meta, expert_in, expert_out, plan, source,
    mixed, moved_in, moved_out,
    T, WI, WO, XY, H, GT, DD, RV, YS, YR, OWN, Q0, Q1, Q2, Q3,
    ld_sem, agr_s, agr_r, agy_s, agy_r, ags_s, ags_r,
    w1x_s, w1x_r, w1y_s, w1y_r, w0y_s, w0y_r, w0x_s, w0x_r,
    sib_s, sib_r, rs_s, rs_r, rsy_s, rsy_r, q1_s, q1_r, q2_s, q2_r,
):
    dp, ex = lax.axis_index("dp"), lax.axis_index("expert")
    x, yl = dp // NYL, dp % NYL
    yh, z, c = ex // (NZ * NC), (ex // NC) % NZ, ex % NC

    def zat(d):
        return (z + d + NZ) % NZ

    def xat(d):
        return ((x + d + NX) % NX) * NYL + yl

    def at_z(d):
        return (dp, (yh * NZ + zat(d)) * NC + c)

    def at_x(d):
        return (xat(d), ex)

    ypart = (dp, ((1 - yh) * NZ + z) * NC + c)
    sibling = (dp, (yh * NZ + z) * NC + 1 - c)
    lpart = (x * NYL + 1 - yl, ex)

    def remote(src, dst, ss, rs, dev):
        return pltpu.make_async_remote_copy(
            src_ref=src, dst_ref=dst, send_sem=ss, recv_sem=rs,
            device_id=dev, device_id_type=MESH,
        )

    sent = {}

    def go(key, cp):
        cp.start()
        sent.setdefault(key, []).append(cp)

    def drain(key):
        for cp in sent.pop(key, []):
            cp.wait_send()

    loads_t = []
    for mb in range(MB):
        loads_t.append((
            pltpu.make_async_copy(tokens.at[mb], T.at[mb, z, yh, c, :, pl.ds(0, D)], ld_sem.at[2 * mb]),
            pltpu.make_async_copy(meta.at[mb], T.at[mb, z, yh, c, :, pl.ds(D, 128)], ld_sem.at[2 * mb + 1]),
        ))
    loads_w = []
    for s in range(2):
        loads_w.append(pltpu.make_async_copy(expert_in.at[0, s], WI.at[s, dp], ld_sem.at[4 + 2 * s]))
        loads_w.append(pltpu.make_async_copy(expert_out.at[0, s], WO.at[s, dp], ld_sem.at[5 + 2 * s]))
    for pair in loads_t:
        for cp in pair:
            cp.start()
    for cp in loads_w:
        cp.start()

    barrier = pltpu.get_barrier_semaphore()

    @pl.loop(1, NEX)
    def _(i):
        pl.semaphore_signal(barrier, inc=1, device_id=(dp, (ex + i) % NEX), device_id_type=MESH)

    for dev in (at_x(1), at_x(-1), lpart):
        pl.semaphore_signal(barrier, inc=1, device_id=dev, device_id_type=MESH)
    pl.semaphore_wait(barrier, NEX - 1 + 3)

    sib_count = [0, 0]

    def chunk(mb, zs, ys):
        return T.at[mb, zs, ys, c]

    def to_sibling(mb, zs, ys):
        k = sib_count[mb]
        sib_count[mb] += 1
        go(("ag", mb), remote(chunk(mb, zs, ys), chunk(mb, zs, ys), ags_s.at[mb, k], ags_r.at[mb, k], sibling))

    def wait_sibling(mb):
        for k in range(NYH * NZ):
            ref = T.at[mb, 0, 0, 0]
            remote(ref, ref, ags_s.at[mb, k], ags_r.at[mb, k], sibling).wait_recv()

    def ring(mb, sgn, d, rel):
        dr = 0 if sgn > 0 else 1
        if d == 3:
            ys = dr
        else:
            ys = yh if rel == 0 else 1 - yh
        ref = chunk(mb, zat(-sgn * d), ys)
        go(("ag", mb), remote(ref, ref, agr_s.at[mb, dr, d, rel], agr_r.at[mb, dr, d, rel], at_z(sgn)))

    def ring_wait(mb, sgn, d, rel):
        dr = 0 if sgn > 0 else 1
        if d == 4:
            ys = dr
        else:
            ys = yh if rel == 0 else 1 - yh
        zs = zat(-sgn * d)
        ref = chunk(mb, zs, ys)
        remote(ref, ref, agr_s.at[mb, dr, d - 1, rel], agr_r.at[mb, dr, d - 1, rel], at_z(sgn)).wait_recv()
        to_sibling(mb, zs, ys)

    def ag_y(mb):
        ref = chunk(mb, z, yh)
        go(("ag", mb), remote(ref, ref, agy_s.at[mb], agy_r.at[mb], ypart))

    def ag_own(mb):
        for sgn in (1, -1):
            ring(mb, sgn, 0, 0)
        to_sibling(mb, z, yh)

    def ag_partner(mb):
        ref = chunk(mb, z, 1 - yh)
        remote(ref, ref, agy_s.at[mb], agy_r.at[mb], ypart).wait_recv()
        for sgn in (1, -1):
            ring(mb, sgn, 0, 1)
        to_sibling(mb, z, 1 - yh)

    def ag_step(mb, d):
        for rel in (0, 1):
            for sgn in (1, -1):
                if d == 4 and rel == 1:
                    continue
                ring_wait(mb, sgn, d, rel)
                if d < 3:
                    ring(mb, sgn, d, rel)
        if d == 3:
            for sgn in (1, -1):
                ring(mb, sgn, 3, 0)

    def wblk(s, b, io, half=None):
        ref = WI if io == 0 else WO
        if half is None:
            return ref.at[s, b]
        rows = (DK if io == 0 else F) // 2
        return ref.at[s, b, pl.ds(half * rows, rows)]

    def wcopy(s, b, io, half, ss, rs, dev):
        ref = wblk(s, b, io, half)
        return remote(ref, ref, ss, rs, dev)

    def w1x(sgn, d):
        dr = 0 if sgn > 0 else 1
        for io in (0, 1):
            half = None if d == 0 else dr
            go("w", wcopy(1, xat(-sgn * d), io, half, w1x_s.at[dr, d, io], w1x_r.at[dr, d, io], at_x(sgn)))

    def w1x_wait(sgn, d):
        dr = 0 if sgn > 0 else 1
        for io in (0, 1):
            half = None if d == 1 else dr
            wcopy(1, xat(-sgn * d), io, half, w1x_s.at[dr, d - 1, io], w1x_r.at[dr, d - 1, io], at_x(sgn)).wait_recv()

    def w1y(k):
        d = (0, 1, -1, 2)[k]
        for io in (0, 1):
            go("w", wcopy(1, xat(d), io, None, w1y_s.at[k, io], w1y_r.at[k, io], lpart))

    def w1y_wait(k):
        d = (0, 1, -1, 2)[k]
        for io in (0, 1):
            b = ((x + d + NX) % NX) * NYL + 1 - yl
            wcopy(1, b, io, None, w1y_s.at[k, io], w1y_r.at[k, io], lpart).wait_recv()

    def w0y():
        for io in (0, 1):
            go("w", wcopy(0, dp, io, None, w0y_s.at[io], w0y_r.at[io], lpart))

    def w0y_wait():
        for io in (0, 1):
            wcopy(0, x * NYL + 1 - yl, io, None, w0y_s.at[io], w0y_r.at[io], lpart).wait_recv()

    def w0blk(d, rel):
        return ((x + d + NX) % NX) * NYL + (yl if rel == 0 else 1 - yl)

    def w0x(sgn, d, rel):
        dr = 0 if sgn > 0 else 1
        for io in (0, 1):
            half = None if d == 0 else dr
            go("w", wcopy(0, w0blk(-sgn * d, rel), io, half, w0x_s.at[dr, d, rel, io], w0x_r.at[dr, d, rel, io], at_x(sgn)))

    def w0x_wait(sgn, d, rel):
        dr = 0 if sgn > 0 else 1
        for io in (0, 1):
            half = None if d == 1 else dr
            wcopy(0, w0blk(-sgn * d, rel), io, half, w0x_s.at[dr, d - 1, rel, io], w0x_r.at[dr, d - 1, rel, io], at_x(sgn)).wait_recv()

    def pack():
        @pl.loop(0, NEX // 2)
        def _(i):
            for h in range(2):
                j = 2 * i + h
                Q0[j, :, 0:512] = WI[1, dp, pl.ds(pl.multiple_of(i * 16, 16), 16), h * 512:(h + 1) * 512]
                Q0[j, :, 512:768] = WO[1, dp, pl.ds(pl.multiple_of(j * 16, 16), 16), :]
        Q1[ex] = Q0[ex]

    def spread(src, dst, ss, rs):
        @pl.loop(1, NEX)
        def _(i):
            j = (ex + i) % NEX
            remote(src.at[j], dst.at[ex], ss.at[i], rs.at[i], (dp, j)).start()

    def spread_wait(src, dst, ss, rs):
        @pl.loop(1, NEX)
        def _(i):
            j = (ex - i + NEX) % NEX
            remote(src.at[j], dst.at[j], ss.at[i], rs.at[i], (dp, j)).wait_recv()

    def spread_drain(src, dst, ss, rs):
        @pl.loop(1, NEX)
        def _(i):
            j = (ex + i) % NEX
            remote(src.at[j], dst.at[ex], ss.at[i], rs.at[i], (dp, j)).wait_send()

    def sort():
        @pl.loop(0, NEX)
        def _(s):
            Q2[s] = Q1[source[s]]
        Q3[ex] = Q2[ex]

    def unpack():
        @pl.loop(0, NEX // 2)
        def _(i):
            for h in range(2):
                j = 2 * i + h
                moved_in[0, pl.ds(pl.multiple_of(i * 16, 16), 16), h * 512:(h + 1) * 512] = Q3[j, :, 0:512]
                moved_out[0, pl.ds(pl.multiple_of(j * 16, 16), 16), :] = Q3[j, :, 512:768]

    def pick(mb):
        @pl.loop(0, NZ)
        def _(g):
            info = T[mb, g, :, :, :, D:WIDE].reshape(GRP, 128).astype(F32).T
            ids, hi, lo = info[0:16], info[16:32], info[32:48]
            names = (ex.astype(F32), (NEX + plan[ex]).astype(F32))
            masks, his, los = [], [], []
            for name in names:
                hit = ids == name
                masks.append(jnp.max(jnp.where(hit, 1.0, 0.0), axis=0, keepdims=True))
                his.append(jnp.sum(jnp.where(hit, hi, 0.0), axis=0, keepdims=True))
                los.append(jnp.sum(jnp.where(hit, lo, 0.0), axis=0, keepdims=True))
            row = lax.broadcasted_iota(jnp.int32, (16, GRP), 0)
            stacked = jnp.where(row == 0, masks[0], jnp.where(row == 1, masks[1], 0.0))
            a = lax.broadcasted_iota(jnp.int32, (GRP, GRP), 0)
            b = lax.broadcasted_iota(jnp.int32, (GRP, GRP), 1)
            before = jnp.where((a // TOK == b // TOK) & (a < b), 1.0, 0.0).astype(BF)
            rank = jnp.dot(stacked.astype(BF), before, preferred_element_type=F32)
            lane = lax.broadcasted_iota(jnp.int32, (1, GRP), 1)
            first = ((lane // TOK) * CAP).astype(F32)
            place = lax.broadcasted_iota(jnp.int32, (ROWS, GRP), 0).astype(F32)
            hot, his_, los_ = [], [], []
            for s in range(2):
                key = jnp.where(masks[s] > 0.0, rank[s:s + 1] + first, -1.0)
                at = place == key
                hot.append(jnp.where(at, 1.0, 0.0))
                his_.append(jnp.where(at, his[s], 0.0))
                los_.append(jnp.where(at, los[s], 0.0))
            back = jnp.concatenate(his_ + los_ + [jnp.zeros((256 - 4 * ROWS, GRP), F32)], axis=0).T
            GT[mb, g] = back.astype(BF).reshape(NYH, NC, TOK, 256)
            pickm = jnp.concatenate(hot, axis=0).astype(BF)
            for n in range(D // NB):
                cols = pl.ds(n * NB, NB)
                tok = T[mb, g, :, :, :, cols].reshape(GRP, NB)
                got = jnp.dot(pickm, tok, preferred_element_type=F32).astype(BF)
                XY[mb, g, :, :, cols] = got.reshape(2, ROWS, NB)

    def ffn(mb, s):
        @pl.loop(0, F // 256)
        def _(n):
            xs = XY[mb, :, s].reshape(NZ * ROWS, D)
            col = pl.multiple_of(n * 256, 256)
            gate = jnp.dot(xs, WI[s, :, :, pl.ds(col, 256)].reshape(D, 256), preferred_element_type=F32)
            up = jnp.dot(xs, WI[s, :, :, pl.ds(col + F, 256)].reshape(D, 256), preferred_element_type=F32)
            H[:, pl.ds(col, 256)] = (gate / (1.0 + jnp.exp(-gate)) * up).astype(BF)

        @pl.loop(0, NDP)
        def _(b):
            y = jnp.dot(H[...], WO[s, b], preferred_element_type=F32).astype(BF)
            XY[mb, :, s, :, pl.ds(pl.multiple_of(b * DK, DK), DK)] = y.reshape(NZ, ROWS, DK)

    def part(mb, zd, core, n):
        cols = pl.ds(pl.multiple_of(n * NB, NB), NB)
        g = GT[mb, zd, :, core].reshape(NYH * TOK, 256)
        y = XY[mb, zd, :, :, cols].reshape(2 * ROWS, NB)
        both = jnp.concatenate([y, y, jnp.zeros((256 - 4 * ROWS, NB), BF)], axis=0)
        return jnp.dot(g, both, preferred_element_type=F32).reshape(NYH, TOK, NB)

    def dref(mb, zd, y, cols=pl.ds(0, D)):
        if mb == 0:
            return DD.at[zd, y, :, cols]
        return T.at[0, zd, y, 0, :, cols]

    def sref(mb, zd, y, cols=pl.ds(0, D)):
        return T.at[mb, zd, y, 1, :, cols]

    def to_sib(mb):
        @pl.loop(0, NZ)
        def _(i):
            mag = 4 - (i + 1) // 2
            zd = zat((2 * (i % 2) - 1) * mag)

            @pl.loop(0, D // NB)
            def _(n):
                cols = pl.ds(pl.multiple_of(n * NB, NB), NB)
                v = part(mb, zd, 1 - c, n).astype(BF)
                for y in range(NYH):
                    sref(mb, zd, y, cols)[...] = v[y]

            for y in range(NYH):
                remote(sref(mb, zd, y), dref(mb, zd, y), sib_s.at[mb, i, y], sib_r.at[mb, i, y], sibling).start()

    def to_sib_drain(mb):
        @pl.loop(0, NZ)
        def _(i):
            mag = 4 - (i + 1) // 2
            zd = zat((2 * (i % 2) - 1) * mag)
            for y in range(NYH):
                remote(sref(mb, zd, y), dref(mb, zd, y), sib_s.at[mb, i, y], sib_r.at[mb, i, y], sibling).wait_send()

    def rs_copy(mb, dr, k, y, zd):
        sgn = 1 if dr == 0 else -1
        return remote(dref(mb, zd, y), RV.at[mb, dr, k, y], rs_s.at[mb, dr, k, y], rs_r.at[mb, dr, k, y], at_z(sgn))

    def rs_step(mb, j):
        for dr in ((0,) if j in (4, 0) else (0, 1)):
            sgn = 1 if dr == 0 else -1
            zd = zat(sgn * j)
            i = 0 if j == 4 else 7 if j == 0 else 2 * (4 - j) - (1 if dr == 0 else 0)
            for y in range(NYH):
                remote(sref(mb, zd, y), dref(mb, zd, y), sib_s.at[mb, i, y], sib_r.at[mb, i, y], sibling).wait_recv()
            arrived = []
            if j < 4:
                for arm in ((0, 1) if j == 0 else (dr,)):
                    for y in ((arm,) if j == 3 else (0, 1)):
                        rs_copy(mb, arm, 3 - j, y, zd).wait_recv()
                        arrived.append((arm, y))

            @pl.loop(0, D // NB)
            def _(n):
                cols = pl.ds(pl.multiple_of(n * NB, NB), NB)
                v = part(mb, zd, c, n)
                for y in range(NYH):
                    acc = v[y] + dref(mb, zd, y, cols)[...].astype(F32)
                    for arm, ya in arrived:
                        if ya == y:
                            acc = acc + RV[mb, arm, 3 - j, y, :, cols].astype(F32)
                    if j == 0:
                        OWN[mb, y, :, cols] = acc
                    else:
                        dref(mb, zd, y, cols)[...] = acc.astype(BF)

            if j == 4:
                go("rs", rs_copy(mb, 0, 0, 0, zd))
                go("rs", rs_copy(mb, 1, 0, 1, zd))
            elif j > 0:
                for y in range(NYH):
                    go("rs", rs_copy(mb, dr, 4 - j, y, zd))
            else:
                YS[mb] = OWN[mb, 1 - yh].astype(BF)
                go("rs", remote(YS.at[mb], YR.at[mb], rsy_s.at[mb], rsy_r.at[mb], ypart))

    def rs_end(mb):
        remote(YS.at[mb], YR.at[mb], rsy_s.at[mb], rsy_r.at[mb], ypart).wait_recv()
        mixed[mb] = (OWN[mb, yh] + YR[mb].astype(F32)).astype(BF)

    for cp in loads_t[0]:
        cp.wait()
    ag_y(0)
    ag_own(0)
    for cp in loads_w:
        cp.wait()
    for sgn in (1, -1):
        w1x(sgn, 0)
    w0y()
    w1y(0)
    for sgn in (1, -1):
        w0x(sgn, 0, 0)
    for cp in loads_t[1]:
        cp.wait()
    ag_y(1)
    ag_partner(0)
    pack()
    ag_step(0, 1)
    w0y_wait()
    for sgn in (1, -1):
        w0x(sgn, 0, 1)
    ag_step(0, 2)
    for k, sgn in ((2, 1), (1, -1)):
        w1x_wait(sgn, 1)
        w1x(sgn, 1)
        w1y(k)
    ag_step(0, 3)
    ag_own(1)
    ag_partner(1)
    for sgn in (1, -1):
        w0x_wait(sgn, 1, 0)
        w0x(sgn, 1, 0)
    ag_step(0, 4)
    ag_step(1, 1)
    for sgn in (1, -1):
        w1x_wait(sgn, 2)
    w1y(3)
    wait_sibling(0)
    pick(0)
    ag_step(1, 2)
    for sgn in (1, -1):
        w0x_wait(sgn, 1, 1)
        w0x(sgn, 1, 1)
    ag_step(1, 3)
    spread(Q0, Q1, q1_s, q1_r)
    ag_step(1, 4)
    for rel in (0, 1):
        for sgn in (1, -1):
            w0x_wait(sgn, 2, rel)
    for k in range(4):
        w1y_wait(k)
    ffn(0, 0)
    ffn(0, 1)
    drain(("ag", 0))
    to_sib(0)
    rs_step(0, 4)
    wait_sibling(1)
    pick(1)
    rs_step(0, 3)
    spread_wait(Q0, Q1, q1_s, q1_r)
    sort()
    spread(Q2, Q3, q2_s, q2_r)
    ffn(1, 0)
    rs_step(0, 2)
    ffn(1, 1)
    drain(("ag", 1))
    rs_step(0, 1)
    to_sib(1)
    rs_step(1, 4)
    rs_step(0, 0)
    rs_step(1, 3)
    spread_wait(Q2, Q3, q2_s, q2_r)
    unpack()
    rs_end(0)
    rs_step(1, 2)
    rs_step(1, 1)
    rs_step(1, 0)
    drain("w")
    spread_drain(Q0, Q1, q1_s, q1_r)
    spread_drain(Q2, Q3, q2_s, q2_r)
    to_sib_drain(0)
    to_sib_drain(1)
    rs_end(1)
    drain("rs")


def on_device(tokens, route_ids, route_gates, expert_in, expert_out, old_plan, new_plan):
    source = jnp.argmax(old_plan[None, :] == new_plan[:, None], axis=1).astype(jnp.int32)
    hi = lax.reduce_precision(route_gates, 8, 7)
    lo = lax.reduce_precision(route_gates - hi, 8, 7)
    fill = ((0, 0), (0, 0), (0, 16 - TOPK))
    meta = jnp.concatenate(
        [
            jnp.pad(route_ids.astype(F32), fill, constant_values=-1.0),
            jnp.pad(hi, fill),
            jnp.pad(lo, fill),
            jnp.zeros((MB, TOK, 128 - 48), F32),
        ],
        axis=2,
    ).astype(BF)
    dma = pltpu.SemaphoreType.DMA
    hbm = pl.BlockSpec(memory_space=pl.ANY)
    smem = pl.BlockSpec(memory_space=pltpu.SMEM)
    vmem = pl.BlockSpec(memory_space=pltpu.VMEM)
    sems = [
        (8,),
        (MB, 2, 4, 2), (MB, 2, 4, 2), (MB,), (MB,), (MB, 16), (MB, 16),
        (2, 2, 2), (2, 2, 2), (4, 2), (4, 2), (2,), (2,), (2, 2, 2, 2), (2, 2, 2, 2),
        (MB, NZ, 2), (MB, NZ, 2), (MB, 2, 4, 2), (MB, 2, 4, 2), (MB,), (MB,),
        (NEX,), (NEX,), (NEX,), (NEX,),
    ]
    return pl.pallas_call(
        kernel,
        out_shape=(
            jax.ShapeDtypeStruct((MB, TOK, D), BF),
            jax.ShapeDtypeStruct((1, DK, 2 * F), BF),
            jax.ShapeDtypeStruct((1, F, DK), BF),
        ),
        in_specs=[hbm, hbm, hbm, hbm, smem, smem],
        out_specs=(vmem, vmem, vmem),
        scratch_shapes=[
            pltpu.VMEM((MB, NZ, NYH, NC, TOK, WIDE), BF),
            pltpu.VMEM((2, NDP, DK, 2 * F), BF),
            pltpu.VMEM((2, NDP, F, DK), BF),
            pltpu.VMEM((MB, NZ, 2, ROWS, D), BF),
            pltpu.VMEM((NZ * ROWS, F), BF),
            pltpu.VMEM((MB, NZ, NYH, NC, TOK, 256), BF),
            pltpu.VMEM((NZ, NYH, TOK, D), BF),
            pltpu.VMEM((MB, 2, 4, NYH, TOK, D), BF),
            pltpu.VMEM((MB, TOK, D), BF),
            pltpu.VMEM((MB, TOK, D), BF),
            pltpu.VMEM((MB, NYH, TOK, D), F32),
            pltpu.VMEM((NEX, 16, 768), BF),
            pltpu.VMEM((NEX, 16, 768), BF),
            pltpu.VMEM((NEX, 16, 768), BF),
            pltpu.VMEM((NEX, 16, 768), BF),
        ]
        + [dma(shape) for shape in sems],
        compiler_params=pltpu.CompilerParams(
            collective_id=0, has_side_effects=True, vmem_limit_bytes=62 * 2**20
        ),
        cost_estimate=pl.CostEstimate(
            flops=MB * 12 * 2**30, bytes_accessed=4 * 2**20, transcendentals=MB * 768 * F
        ),
    )(tokens, meta, expert_in, expert_out, old_plan, source)


def solution(mesh):
    in_specs = (
        P(None, ("dp", "expert"), None),
        P(None, ("dp", "expert"), None),
        P(None, ("dp", "expert"), None),
        P("expert", None, "dp", None),
        P("expert", None, None, "dp"),
        P(),
        P(),
    )
    out_specs = (P(None, ("dp", "expert"), None), P("expert", "dp", None), P("expert", None, "dp"))
    return jax.shard_map(
        on_device, mesh=mesh, in_specs=in_specs, out_specs=out_specs, check_vma=False
    )
```

time: 722 us -> 251 us (0.35)
  waiting for transfers between devices: 379 us -> 0 us
  Pallas kernels: 0 us -> 239 us
  local copies, waits for them, and re-layouts: 192 us -> 4.7 us
  starting transfers between devices: 73.3 us -> 0 us
  matrix products: 32.1 us -> 0 us
  other arithmetic: 20.7 us -> 2.14 us
  between operations: 14.6 us -> 0.69 us
    all_gather x4 -> x0, waiting for transfers between devices: 253 us -> none  [the longest x1 110 us: on_device(): lax.all_gather(expert_out, 'dp', axis=3, tiled=True)]
    pallas_call x0 -> x1, Pallas kernels: none -> 239 us  [on_device(): pl.pallas_call(kernel, out_shape=(jax.ShapeDtypeStruct((MB, TOK, D), BF),...]
    all_to_all x8 -> x0, waiting for transfers between devices: 124 us -> none  [the longest x2 55.1 us: micro_batch(): lax.all_to_all(jnp.stack(results, axis=1), 'expert', split_axis=0, concat...]
    all_to_all x8 -> x0, starting transfers between devices: 73.1 us -> none  [the longest x2 21.7 us: micro_batch(): lax.all_to_all(jnp.stack(results, axis=1), 'expert', split_axis=0, concat...]
    reshape x8 -> x0, local copies, waits for them, and re-layouts: 43.5 us -> none  [the longest x4 23 us: micro_batch(): outgoing.reshape(groups, 2, capacity, width)]
    slice x4 -> x0, local copies, waits for them, and re-layouts: 35.6 us -> none  [the longest x2 35.6 us: micro_batch(): picked = arrived[:, slot_index].reshape(groups * capacity, width)]
    another operation x10 -> x1, local copies, waits for them, and re-layouts: 35.5 us -> 0.12 us  [the longest x6 23.1 us: micro_batch(): jnp.stack(results, axis=1)]
    dot_general x10 -> x0, matrix products: 32.1 us -> none  [the longest x4 19.3 us: expert_apply(): projected = jnp.dot(picked, weight_in, preferred_element_type=jnp.float32)]
  transfers between devices with their start and end apart: 12 -> 0, of which waited for: 9 -> 0; matrix products, arithmetic and copies ran while one was open for 30% -> 0% of each run, Pallas kernels for 0% -> 0%
where the time goes in v1:
time: 251 us; the launch traced here: 247 us
  Pallas kernels  239 us (95%)
  local copies, waits for them, and re-layouts  4.7 us (2%)
    pallas_call x1, Pallas kernels, on_device(): pl.pallas_call(kernel, out_shape=(jax.ShapeDtypeStruct((MB, TOK, D), BF),...  239 us

profile of v1, /device:TPU:1, one launch (start us, length us, event | category | flops | bytes accessed | tf_op | source)
XLA Modules:
  0.0 246.6 jit_solution(6550184648594087022)
XLA Ops:
  0.6 0.0 copy-start.3
  0.6 0.0 copy-start.4
  0.7 0.0 copy-start.2
  0.7 0.1 pad.20.clone
  0.8 0.5 copy-done.3
  1.3 0.0 copy-done.4
  1.3 0.7 iota_reduce_fusion
  2.0 0.7 convert_convert_fusion
  2.7 0.0 copy-done.2
  2.7 0.1 copy.16
  2.8 0.1 copy.17
  2.9 0.1 copy.18
  3.1 0.7 fusion.6.meta
  3.8 239.1 %shard_map.94 = (bf16[2,64,2048]{2,1,0:T(8,128)(2,1)}, bf16[1,256,1024]{2,1,0:T(8,128)(2,1)}, bf16[1,512,256]{2,1,0:T(8,128)(2,1)}) custom-call(bf16[2,64,2048]{2,1,0:T(8,128)(2,1)} %tokens.1, bf16[2,64,128]{2,1,0:T(8,128)(2,1)} %fusion.6.meta, bf16[1,2,256,1024]{3,2,1,0:T(8,128)(2,1)} %expert_in.1, bf16[1,2,512,256]{3,2,1,0:T(8,128)(2,1)} %expert_out.1, ...), custom_call_target="tpu_custom_call" | custom-call | flops 25769803776 | bytes 4194304 | tf_op jit(solution)/shard_map/pallas_call | solution.py:498
  242.9 0.0 copy-start
  242.9 1.9 copy.23
  244.8 0.0 copy-done
  244.8 0.0 copy-start.1
  244.8 0.8 copy.24
  245.6 0.3 copy-done.1
  245.9 0.7 copy.25
  (3 shorter events, 0.0 us)
Async XLA Ops:
  0.6 0.7 copy-start.3
  0.6 0.7 copy-start.4
  0.7 2.1 copy-start.2
  242.9 2.0 copy-start
  244.8 1.1 copy-start.1

commit v2 on v1

--- a/solution.py
+++ b/solution.py
@@ -20,12 +20,13 @@
 def kernel(
     tokens, meta, expert_in, expert_out, plan, source,
     mixed, moved_in, moved_out,
-    T, WI, WO, XY, H, GT, DD, RV, YS, YR, OWN, Q0, Q1, Q2, Q3,
+    T0, T1, WI, WO, XY, H, GT, DD, RV, YS, YR, OWN, PRE, Q0, Q1, Q2, Q3,
     ld_sem, agr_s, agr_r, agy_s, agy_r, ags_s, ags_r,
     w1x_s, w1x_r, w1y_s, w1y_r, w0y_s, w0y_r, w0x_s, w0x_r,
-    sib_s, sib_r, rs_s, rs_r, rsy_s, rsy_r, q1_s, q1_r, q2_s, q2_r,
+    sib_s, sib_r, rs_s, rs_r, rsy_s, rsy_r, cr_s, cr_r, q1_s, q1_r, q2_s, q2_r,
 ):
     dp, ex = lax.axis_index("dp"), lax.axis_index("expert")
+    T = (T0, T1)
     x, yl = dp // NYL, dp % NYL
     yh, z, c = ex // (NZ * NC), (ex // NC) % NZ, ex % NC
 
@@ -61,12 +62,13 @@
         for cp in sent.pop(key, []):
             cp.wait_send()
 
-    loads_t = []
-    for mb in range(MB):
-        loads_t.append((
-            pltpu.make_async_copy(tokens.at[mb], T.at[mb, z, yh, c, :, pl.ds(0, D)], ld_sem.at[2 * mb]),
-            pltpu.make_async_copy(meta.at[mb], T.at[mb, z, yh, c, :, pl.ds(D, 128)], ld_sem.at[2 * mb + 1]),
-        ))
+    loads_t = [
+        (
+            pltpu.make_async_copy(tokens.at[0], T0.at[z, yh, c, :, pl.ds(0, D)], ld_sem.at[0]),
+            pltpu.make_async_copy(meta, T0.at[z, yh, c, :, pl.ds(D, 128)], ld_sem.at[1]),
+        ),
+        (pltpu.make_async_copy(tokens.at[1], T1.at[z, yh, c], ld_sem.at[2]),),
+    ]
     loads_w = []
     for s in range(2):
         loads_w.append(pltpu.make_async_copy(expert_in.at[0, s], WI.at[s, dp], ld_sem.at[4 + 2 * s]))
@@ -79,18 +81,14 @@
 
     barrier = pltpu.get_barrier_semaphore()
 
-    @pl.loop(1, NEX)
-    def _(i):
-        pl.semaphore_signal(barrier, inc=1, device_id=(dp, (ex + i) % NEX), device_id_type=MESH)
-
-    for dev in (at_x(1), at_x(-1), lpart):
+    for dev in (at_z(1), at_z(-1), ypart, sibling, lpart, at_x(1), at_x(-1)):
         pl.semaphore_signal(barrier, inc=1, device_id=dev, device_id_type=MESH)
-    pl.semaphore_wait(barrier, NEX - 1 + 3)
+    pl.semaphore_wait(barrier, 7)
 
     sib_count = [0, 0]
 
     def chunk(mb, zs, ys):
-        return T.at[mb, zs, ys, c]
+        return T[mb].at[zs, ys, c]
 
     def to_sibling(mb, zs, ys):
         k = sib_count[mb]
@@ -99,7 +97,7 @@
 
     def wait_sibling(mb):
         for k in range(NYH * NZ):
-            ref = T.at[mb, 0, 0, 0]
+            ref = T[mb].at[0, 0, 0]
             remote(ref, ref, ags_s.at[mb, k], ags_r.at[mb, k], sibling).wait_recv()
 
     def ring(mb, sgn, d, rel):
@@ -150,6 +148,8 @@
             for sgn in (1, -1):
                 ring(mb, sgn, 3, 0)
 
+    x_first, y_first = [(1, 0)], [(0, 0), (0, 1), (1, 1)]
+
     def wblk(s, b, io, half=None):
         ref = WI if io == 0 else WO
         if half is None:
@@ -163,49 +163,49 @@
 
     def w1x(sgn, d):
         dr = 0 if sgn > 0 else 1
-        for io in (0, 1):
+        for q, (s, io) in enumerate(x_first):
             half = None if d == 0 else dr
-            go("w", wcopy(1, xat(-sgn * d), io, half, w1x_s.at[dr, d, io], w1x_r.at[dr, d, io], at_x(sgn)))
+            go("w", wcopy(s, xat(-sgn * d), io, half, w1x_s.at[dr, d, q], w1x_r.at[dr, d, q], at_x(sgn)))
 
     def w1x_wait(sgn, d):
         dr = 0 if sgn > 0 else 1
-        for io in (0, 1):
+        for q, (s, io) in enumerate(x_first):
             half = None if d == 1 else dr
-            wcopy(1, xat(-sgn * d), io, half, w1x_s.at[dr, d - 1, io], w1x_r.at[dr, d - 1, io], at_x(sgn)).wait_recv()
+            wcopy(s, xat(-sgn * d), io, half, w1x_s.at[dr, d - 1, q], w1x_r.at[dr, d - 1, q], at_x(sgn)).wait_recv()
 
     def w1y(k):
         d = (0, 1, -1, 2)[k]
-        for io in (0, 1):
-            go("w", wcopy(1, xat(d), io, None, w1y_s.at[k, io], w1y_r.at[k, io], lpart))
+        for q, (s, io) in enumerate(x_first):
+            go("w", wcopy(s, xat(d), io, None, w1y_s.at[k, q], w1y_r.at[k, q], lpart))
 
     def w1y_wait(k):
         d = (0, 1, -1, 2)[k]
-        for io in (0, 1):
+        for q, (s, io) in enumerate(x_first):
             b = ((x + d + NX) % NX) * NYL + 1 - yl
-            wcopy(1, b, io, None, w1y_s.at[k, io], w1y_r.at[k, io], lpart).wait_recv()
+            wcopy(s, b, io, None, w1y_s.at[k, q], w1y_r.at[k, q], lpart).wait_recv()
 
     def w0y():
-        for io in (0, 1):
-            go("w", wcopy(0, dp, io, None, w0y_s.at[io], w0y_r.at[io], lpart))
+        for q, (s, io) in enumerate(y_first):
+            go("w", wcopy(s, dp, io, None, w0y_s.at[q], w0y_r.at[q], lpart))
 
     def w0y_wait():
-        for io in (0, 1):
-            wcopy(0, x * NYL + 1 - yl, io, None, w0y_s.at[io], w0y_r.at[io], lpart).wait_recv()
+        for q, (s, io) in enumerate(y_first):
+            wcopy(s, x * NYL + 1 - yl, io, None, w0y_s.at[q], w0y_r.at[q], lpart).wait_recv()
 
     def w0blk(d, rel):
         return ((x + d + NX) % NX) * NYL + (yl if rel == 0 else 1 - yl)
 
     def w0x(sgn, d, rel):
         dr = 0 if sgn > 0 else 1
-        for io in (0, 1):
+        for q, (s, io) in enumerate(y_first):
             half = None if d == 0 else dr
-            go("w", wcopy(0, w0blk(-sgn * d, rel), io, half, w0x_s.at[dr, d, rel, io], w0x_r.at[dr, d, rel, io], at_x(sgn)))
+            go("w", wcopy(s, w0blk(-sgn * d, rel), io, half, w0x_s.at[dr, d, rel, q], w0x_r.at[dr, d, rel, q], at_x(sgn)))
 
     def w0x_wait(sgn, d, rel):
         dr = 0 if sgn > 0 else 1
-        for io in (0, 1):
+        for q, (s, io) in enumerate(y_first):
             half = None if d == 1 else dr
-            wcopy(0, w0blk(-sgn * d, rel), io, half, w0x_s.at[dr, d - 1, rel, io], w0x_r.at[dr, d - 1, rel, io], at_x(sgn)).wait_recv()
+            wcopy(s, w0blk(-sgn * d, rel), io, half, w0x_s.at[dr, d - 1, rel, q], w0x_r.at[dr, d - 1, rel, q], at_x(sgn)).wait_recv()
 
     def pack():
         @pl.loop(0, NEX // 2)
@@ -251,8 +251,10 @@
     def pick(mb):
         @pl.loop(0, NZ)
         def _(g):
-            info = T[mb, g, :, :, :, D:WIDE].reshape(GRP, 128).astype(F32).T
-            ids, hi, lo = info[0:16], info[16:32], info[32:48]
+            info = jnp.concatenate(
+                [T0[g, ys, :, :, D:WIDE].reshape(GRP // 2, 128) for ys in (yh, 1 - yh)], axis=0
+            ).astype(F32).T
+            ids, hi, lo = (info[48 * mb + k:48 * mb + k + 16] for k in (0, 16, 32))
             names = (ex.astype(F32), (NEX + plan[ex]).astype(F32))
             masks, his, los = [], [], []
             for name in names:
@@ -281,7 +283,9 @@
             pickm = jnp.concatenate(hot, axis=0).astype(BF)
             for n in range(D // NB):
                 cols = pl.ds(n * NB, NB)
-                tok = T[mb, g, :, :, :, cols].reshape(GRP, NB)
+                tok = jnp.concatenate(
+                    [T[mb][g, ys, :, :, cols].reshape(GRP // 2, NB) for ys in (yh, 1 - yh)], axis=0
+                )
                 got = jnp.dot(pickm, tok, preferred_element_type=F32).astype(BF)
                 XY[mb, g, :, :, cols] = got.reshape(2, ROWS, NB)
 
@@ -299,90 +303,149 @@
             y = jnp.dot(H[...], WO[s, b], preferred_element_type=F32).astype(BF)
             XY[mb, :, s, :, pl.ds(pl.multiple_of(b * DK, DK), DK)] = y.reshape(NZ, ROWS, DK)
 
-    def part(mb, zd, core, n):
+    def part(mb, zd, core, rels, n):
         cols = pl.ds(pl.multiple_of(n * NB, NB), NB)
-        g = GT[mb, zd, :, core].reshape(NYH * TOK, 256)
+        if len(rels) == 2:
+            g = GT[mb, zd, :, core].reshape(NYH * TOK, 256)
+        else:
+            g = GT[mb, zd, rels[0], core]
         y = XY[mb, zd, :, :, cols].reshape(2 * ROWS, NB)
         both = jnp.concatenate([y, y, jnp.zeros((256 - 4 * ROWS, NB), BF)], axis=0)
-        return jnp.dot(g, both, preferred_element_type=F32).reshape(NYH, TOK, NB)
-
-    def dref(mb, zd, y, cols=pl.ds(0, D)):
+        return jnp.dot(g, both, preferred_element_type=F32).reshape(len(rels), TOK, NB)
+
+    def dref(mb, zd, rel, cols=pl.ds(0, D)):
         if mb == 0:
-            return DD.at[zd, y, :, cols]
-        return T.at[0, zd, y, 0, :, cols]
-
-    def sref(mb, zd, y, cols=pl.ds(0, D)):
-        return T.at[mb, zd, y, 1, :, cols]
-
-    def to_sib(mb):
-        @pl.loop(0, NZ)
+            return DD.at[zd, rel, :, cols]
+        return T0.at[zd, rel, 0, :, cols]
+
+    def sref(mb, zd, rel, cols=pl.ds(0, D)):
+        return T[mb].at[zd, rel, 1, :, cols]
+
+    def sib_copy(mb, i, rel, zd):
+        return remote(sref(mb, zd, rel), dref(mb, zd, rel), sib_s.at[mb, i, rel], sib_r.at[mb, i, rel], sibling)
+
+    def turn(i):
+        return zat((2 * (i % 2) - 1) * (4 - (i + 1) // 2))
+
+    def to_sib(mb, lo, hi):
+        @pl.loop(lo, hi)
         def _(i):
-            mag = 4 - (i + 1) // 2
-            zd = zat((2 * (i % 2) - 1) * mag)
+            zd = turn(i)
 
             @pl.loop(0, D // NB)
             def _(n):
                 cols = pl.ds(pl.multiple_of(n * NB, NB), NB)
-                v = part(mb, zd, 1 - c, n).astype(BF)
-                for y in range(NYH):
-                    sref(mb, zd, y, cols)[...] = v[y]
-
-            for y in range(NYH):
-                remote(sref(mb, zd, y), dref(mb, zd, y), sib_s.at[mb, i, y], sib_r.at[mb, i, y], sibling).start()
+                v = part(mb, zd, 1 - c, (0, 1), n).astype(BF)
+                for rel in range(2):
+                    sref(mb, zd, rel, cols)[...] = v[rel]
+
+            for rel in range(2):
+                sib_copy(mb, i, rel, zd).start()
 
     def to_sib_drain(mb):
         @pl.loop(0, NZ)
         def _(i):
-            mag = 4 - (i + 1) // 2
-            zd = zat((2 * (i % 2) - 1) * mag)
-            for y in range(NYH):
-                remote(sref(mb, zd, y), dref(mb, zd, y), sib_s.at[mb, i, y], sib_r.at[mb, i, y], sibling).wait_send()
-
-    def rs_copy(mb, dr, k, y, zd):
-        sgn = 1 if dr == 0 else -1
-        return remote(dref(mb, zd, y), RV.at[mb, dr, k, y], rs_s.at[mb, dr, k, y], rs_r.at[mb, dr, k, y], at_z(sgn))
-
-    def rs_step(mb, j):
-        for dr in ((0,) if j in (4, 0) else (0, 1)):
-            sgn = 1 if dr == 0 else -1
-            zd = zat(sgn * j)
-            i = 0 if j == 4 else 7 if j == 0 else 2 * (4 - j) - (1 if dr == 0 else 0)
-            for y in range(NYH):
-                remote(sref(mb, zd, y), dref(mb, zd, y), sib_s.at[mb, i, y], sib_r.at[mb, i, y], sibling).wait_recv()
-            arrived = []
-            if j < 4:
-                for arm in ((0, 1) if j == 0 else (dr,)):
-                    for y in ((arm,) if j == 3 else (0, 1)):
-                        rs_copy(mb, arm, 3 - j, y, zd).wait_recv()
-                        arrived.append((arm, y))
-
-            @pl.loop(0, D // NB)
-            def _(n):
-                cols = pl.ds(pl.multiple_of(n * NB, NB), NB)
-                v = part(mb, zd, c, n)
-                for y in range(NYH):
-                    acc = v[y] + dref(mb, zd, y, cols)[...].astype(F32)
-                    for arm, ya in arrived:
-                        if ya == y:
-                            acc = acc + RV[mb, arm, 3 - j, y, :, cols].astype(F32)
-                    if j == 0:
-                        OWN[mb, y, :, cols] = acc
-                    else:
-                        dref(mb, zd, y, cols)[...] = acc.astype(BF)
-
-            if j == 4:
-                go("rs", rs_copy(mb, 0, 0, 0, zd))
-                go("rs", rs_copy(mb, 1, 0, 1, zd))
-            elif j > 0:
-                for y in range(NYH):
-                    go("rs", rs_copy(mb, dr, 4 - j, y, zd))
-            else:
-                YS[mb] = OWN[mb, 1 - yh].astype(BF)
-                go("rs", remote(YS.at[mb], YR.at[mb], rsy_s.at[mb], rsy_r.at[mb], ypart))
+            for rel in range(2):
+                sib_copy(mb, i, rel, turn(i)).wait_send()
+
+    def half(h):
+        return pl.ds(h * (TOK // 2), TOK // 2)
+
+    def rs_copy(mb, dr, k, rel, h, zd):
+        return remote(
+            dref(mb, zd, rel).at[half(h)], RV.at[mb, dr, k, rel, half(h)],
+            rs_s.at[mb, dr, k, rel, h], rs_r.at[mb, dr, k, rel, h], at_z(1 if dr == 0 else -1),
+        )
+
+    def cross_slot(mb, i):
+        return RV.at[mb, (0, 0, 1)[i], (0, 1, 1)[i], 1]
+
+    def cross_copy(mb, i, h, zd):
+        return remote(
+            dref(mb, zd, 1).at[half(h)], cross_slot(mb, i).at[half(h)],
+            cr_s.at[mb, i, h], cr_r.at[mb, i, h], ypart,
+        )
+
+    def home_copy(mb, h):
+        return remote(YS.at[mb, half(h)], YR.at[mb, half(h)], rsy_s.at[mb, h], rsy_r.at[mb, h], ypart)
+
+    def pre(slot, mb, zd, i, rel):
+        sib_copy(mb, i, rel, zd).wait_recv()
+
+        @pl.loop(0, D // NB)
+        def _(n):
+            cols = pl.ds(pl.multiple_of(n * NB, NB), NB)
+            PRE[slot, :, cols] = part(mb, zd, c, (rel,), n)[0] + dref(mb, zd, rel, cols)[...].astype(F32)
+
+    def put(slot, h, arrived, out):
+        @pl.loop(0, D // NB)
+        def _(n):
+            cols = pl.ds(pl.multiple_of(n * NB, NB), NB)
+            acc = PRE[slot, half(h), cols]
+            for ref in arrived:
+                acc = acc + ref[half(h), cols].astype(F32)
+            out.at[half(h), cols][...] = acc.astype(out.dtype)
+
+    def cross(mb, i):
+        zd = turn(i)
+        pre(0, mb, zd, i, 1)
+        for h in (0, 1):
+            put(0, h, [], dref(mb, zd, 1))
+            go("rs", cross_copy(mb, i, h, zd))
+
+    def rs_other(mb, j):
+        at = [(dr, 2 * (4 - j) - 1 + dr, turn(2 * (4 - j) - 1 + dr)) for dr in (0, 1)]
+        for dr, i, zd in at:
+            pre(dr, mb, zd, i, 1)
+        for h in (0, 1):
+            for dr, i, zd in at:
+                arrived = []
+                if j == 1:
+                    rs_copy(mb, dr, 2, 1, h, zd).wait_recv()
+                    arrived.append(RV.at[mb, dr, 2, 1])
+                put(dr, h, arrived, dref(mb, zd, 1))
+                go("rs", rs_copy(mb, dr, 4 - j, 1, h, zd))
+
+    def rs_far(mb):
+        zd = turn(0)
+        pre(0, mb, zd, 0, 0)
+        for h in (0, 1):
+            cross_copy(mb, 0, h, zd).wait_recv()
+            put(0, h, [cross_slot(mb, 0)], dref(mb, zd, 0))
+            go("rs", rs_copy(mb, h, 0, 0, h, zd))
+
+    def rs_own(mb, j):
+        at = [(dr, 2 * (4 - j) - 1 + dr, turn(2 * (4 - j) - 1 + dr)) for dr in (0, 1)]
+        for dr, i, zd in at:
+            pre(dr, mb, zd, i, 0)
+        for turn_h in (0, 1):
+            for dr, i, zd in at:
+                h = turn_h if dr == 1 else 1 - turn_h
+                arrived = []
+                if j == 3:
+                    cross_copy(mb, i, h, zd).wait_recv()
+                    arrived.append(cross_slot(mb, i))
+                if j < 3 or h == dr:
+                    rs_copy(mb, dr, 3 - j, 0, h, zd).wait_recv()
+                    arrived.append(RV.at[mb, dr, 3 - j, 0])
+                put(dr, h, arrived, dref(mb, zd, 0))
+                go("rs", rs_copy(mb, dr, 4 - j, 0, h, zd))
+
+    def rs_home(mb):
+        for rel in (1, 0):
+            pre(rel, mb, z, 7, rel)
+        for rel in (1, 0):
+            for h in (0, 1):
+                for arm in (0, 1):
+                    rs_copy(mb, arm, 3, rel, h, z).wait_recv()
+                put(rel, h, [RV.at[mb, arm, 3, rel] for arm in (0, 1)], (OWN if rel == 0 else YS).at[mb])
+                if rel == 1:
+                    go("rs", home_copy(mb, h))
 
     def rs_end(mb):
-        remote(YS.at[mb], YR.at[mb], rsy_s.at[mb], rsy_r.at[mb], ypart).wait_recv()
-        mixed[mb] = (OWN[mb, yh] + YR[mb].astype(F32)).astype(BF)
+        for h in (0, 1):
+            home_copy(mb, h).wait_recv()
+            mixed[mb, half(h)] = (OWN[mb, half(h)] + YR[mb, half(h)].astype(F32)).astype(BF)
 
     for cp in loads_t[0]:
         cp.wait()
@@ -438,29 +501,44 @@
     ffn(0, 0)
     ffn(0, 1)
     drain(("ag", 0))
-    to_sib(0)
-    rs_step(0, 4)
+    def rs_first(mb):
+        to_sib(mb, 0, 1)
+        cross(mb, 0)
+        to_sib(mb, 1, 3)
+        cross(mb, 1)
+        cross(mb, 2)
+        to_sib(mb, 3, 5)
+        rs_other(mb, 2)
+        rs_far(mb)
+
+    def rs_second(mb):
+        to_sib(mb, 5, 7)
+        rs_other(mb, 1)
+        rs_own(mb, 3)
+
+    rs_first(0)
     wait_sibling(1)
     pick(1)
-    rs_step(0, 3)
+    rs_second(0)
     spread_wait(Q0, Q1, q1_s, q1_r)
     sort()
     spread(Q2, Q3, q2_s, q2_r)
     ffn(1, 0)
-    rs_step(0, 2)
     ffn(1, 1)
+    rs_own(0, 2)
     drain(("ag", 1))
-    rs_step(0, 1)
-    to_sib(1)
-    rs_step(1, 4)
-    rs_step(0, 0)
-    rs_step(1, 3)
+    rs_first(1)
+    to_sib(0, 7, 8)
+    rs_own(0, 1)
+    rs_second(1)
+    rs_home(0)
+    rs_own(1, 2)
+    rs_end(0)
+    to_sib(1, 7, 8)
+    rs_own(1, 1)
     spread_wait(Q2, Q3, q2_s, q2_r)
     unpack()
-    rs_end(0)
-    rs_step(1, 2)
-    rs_step(1, 1)
-    rs_step(1, 0)
+    rs_home(1)
     drain("w")
     spread_drain(Q0, Q1, q1_s, q1_r)
     spread_drain(Q2, Q3, q2_s, q2_r)
@@ -474,16 +552,14 @@
     source = jnp.argmax(old_plan[None, :] == new_plan[:, None], axis=1).astype(jnp.int32)
     hi = lax.reduce_precision(route_gates, 8, 7)
     lo = lax.reduce_precision(route_gates - hi, 8, 7)
-    fill = ((0, 0), (0, 0), (0, 16 - TOPK))
-    meta = jnp.concatenate(
-        [
-            jnp.pad(route_ids.astype(F32), fill, constant_values=-1.0),
-            jnp.pad(hi, fill),
-            jnp.pad(lo, fill),
-            jnp.zeros((MB, TOK, 128 - 48), F32),
-        ],
-        axis=2,
-    ).astype(BF)
+    fill = ((0, 0), (0, 16 - TOPK))
+    parts = []
+    for mb in range(MB):
+        parts.append(jnp.pad(route_ids[mb].astype(F32), fill, constant_values=-1.0))
+        parts.append(jnp.pad(hi[mb], fill))
+        parts.append(jnp.pad(lo[mb], fill))
+    parts.append(jnp.zeros((TOK, 128 - 48 * MB), F32))
+    meta = jnp.concatenate(parts, axis=1).astype(BF)
     dma = pltpu.SemaphoreType.DMA
     hbm = pl.BlockSpec(memory_space=pl.ANY)
     smem = pl.BlockSpec(memory_space=pltpu.SMEM)
@@ -491,8 +567,8 @@
     sems = [
         (8,),
         (MB, 2, 4, 2), (MB, 2, 4, 2), (MB,), (MB,), (MB, 16), (MB, 16),
-        (2, 2, 2), (2, 2, 2), (4, 2), (4, 2), (2,), (2,), (2, 2, 2, 2), (2, 2, 2, 2),
-        (MB, NZ, 2), (MB, NZ, 2), (MB, 2, 4, 2), (MB, 2, 4, 2), (MB,), (MB,),
+        (2, 2, 1), (2, 2, 1), (4, 1), (4, 1), (3,), (3,), (2, 2, 2, 3), (2, 2, 2, 3),
+        (MB, NZ, 2), (MB, NZ, 2), (MB, 2, 4, 2, 2), (MB, 2, 4, 2, 2), (MB, 2), (MB, 2), (MB, 3, 2), (MB, 3, 2),
         (NEX,), (NEX,), (NEX,), (NEX,),
     ]
     return pl.pallas_call(
@@ -505,7 +581,8 @@
         in_specs=[hbm, hbm, hbm, hbm, smem, smem],
         out_specs=(vmem, vmem, vmem),
         scratch_shapes=[
-            pltpu.VMEM((MB, NZ, NYH, NC, TOK, WIDE), BF),
+            pltpu.VMEM((NZ, NYH, NC, TOK, WIDE), BF),
+            pltpu.VMEM((NZ, NYH, NC, TOK, D), BF),
             pltpu.VMEM((2, NDP, DK, 2 * F), BF),
             pltpu.VMEM((2, NDP, F, DK), BF),
             pltpu.VMEM((MB, NZ, 2, ROWS, D), BF),
@@ -515,7 +592,8 @@
             pltpu.VMEM((MB, 2, 4, NYH, TOK, D), BF),
             pltpu.VMEM((MB, TOK, D), BF),
             pltpu.VMEM((MB, TOK, D), BF),
-            pltpu.VMEM((MB, NYH, TOK, D), F32),
+            pltpu.VMEM((MB, TOK, D), F32),
+            pltpu.VMEM((2, TOK, D), F32),
             pltpu.VMEM((NEX, 16, 768), BF),
             pltpu.VMEM((NEX, 16, 768), BF),
             pltpu.VMEM((NEX, 16, 768), BF),

time: 251 us -> 226 us (0.900); the launches traced: 247 us -> 226 us
  Pallas kernels: 239 us -> 217 us
    pallas_call x1, Pallas kernels: 239 us -> 217 us  [on_device(): pl.pallas_call(kernel, out_shape=(jax.ShapeDtypeStruct((MB, TOK, D), BF),...]
where the time goes in v2:
time: 226 us
  Pallas kernels  217 us (96%)
  local copies, waits for them, and re-layouts  6.27 us (3%)
    pallas_call x1, Pallas kernels, on_device(): pl.pallas_call(kernel, out_shape=(jax.ShapeDtypeStruct((MB, TOK, D), BF),...  217 us
    unnamed x12, local copies, waits for them, and re-layouts  4.7 us

profile of v2, /device:TPU:1, one launch (start us, length us, event | category | flops | bytes accessed | tf_op | source)
XLA Modules:
  0.0 225.7 jit_solution(5299982619949003893)
XLA Ops:
  0.6 1.4 iota_reduce_fusion
  2.0 0.8 fusion.4
  2.8 0.1 copy.19
  2.9 0.1 copy.18
  3.0 0.0 copy-start.2
  3.0 0.7 copy-done.2
  3.7 0.1 copy.15
  3.9 0.7 concatenate.4.meta
  4.6 217.3 %shard_map.94 = (bf16[2,64,2048]{2,1,0:T(8,128)(2,1)}, bf16[1,256,1024]{2,1,0:T(8,128)(2,1)}, bf16[1,512,256]{2,1,0:T(8,128)(2,1)}) custom-call(bf16[2,64,2048]{2,1,0:T(8,128)(2,1)} %tokens.1, bf16[64,128]{1,0:T(8,128)(2,1)} %concatenate.4.meta, bf16[1,2,256,1024]{3,2,1,0:T(8,128)(2,1)} %expert_in.1, bf16[1,2,512,256]{3,2,1,0:T(8,128)(2,1)} %expert_out.1, ...), custom_call_target="tpu_custom_call" | custom-call | flops 25769803776 | bytes 4194304 | tf_op jit(solution)/shard_map/pallas_call | solution.py:574
  221.9 0.0 copy-start
  221.9 1.9 copy.23
  223.9 0.0 copy-done
  223.9 0.0 copy-start.1
  223.9 0.8 copy.24
  224.7 0.3 copy-done.1
  225.0 0.7 copy.25
  (11 shorter events, 0.1 us)
Async XLA Ops:
  3.0 0.7 copy-start.2
  221.9 2.0 copy-start
  223.9 1.1 copy-start.1

commit v3 on v2

--- a/solution.py
+++ b/solution.py
@@ -14,13 +14,14 @@
 ROWS = NYH * NC * CAP
 WIDE = D + 128
 NB = 512
+PZ = 4
 BF, F32 = jnp.bfloat16, jnp.float32
 
 
 def kernel(
-    tokens, meta, expert_in, expert_out, plan, source,
+    tokens, route_ids, route_gates, expert_in, expert_out, plan, new_plan,
     mixed, moved_in, moved_out,
-    T0, T1, WI, WO, XY, H, GT, DD, RV, YS, YR, OWN, PRE, Q0, Q1, Q2, Q3,
+    T0, T1, WI, WO, XY, H, GT, DD, RV, YS, YR, OWN, PRE, Q0, Q1, Q2, Q3, source,
     ld_sem, agr_s, agr_r, agy_s, agy_r, ags_s, ags_r,
     w1x_s, w1x_r, w1y_s, w1y_r, w0y_s, w0y_r, w0x_s, w0x_r,
     sib_s, sib_r, rs_s, rs_r, rsy_s, rsy_r, cr_s, cr_r, q1_s, q1_r, q2_s, q2_r,
@@ -63,10 +64,7 @@
             cp.wait_send()
 
     loads_t = [
-        (
-            pltpu.make_async_copy(tokens.at[0], T0.at[z, yh, c, :, pl.ds(0, D)], ld_sem.at[0]),
-            pltpu.make_async_copy(meta, T0.at[z, yh, c, :, pl.ds(D, 128)], ld_sem.at[1]),
-        ),
+        (pltpu.make_async_copy(tokens.at[0], T0.at[z, yh, c, :, pl.ds(0, D)], ld_sem.at[0]),),
         (pltpu.make_async_copy(tokens.at[1], T1.at[z, yh, c], ld_sem.at[2]),),
     ]
     loads_w = []
@@ -83,6 +81,14 @@
 
     for dev in (at_z(1), at_z(-1), ypart, sibling, lpart, at_x(1), at_x(-1)):
         pl.semaphore_signal(barrier, inc=1, device_id=dev, device_id_type=MESH)
+
+    T0[z, yh, c, :, D:WIDE] = jnp.full((TOK, WIDE - D), -1.0, BF)
+    for mb in range(MB):
+        hi = route_gates[mb].astype(BF)
+        lo = (route_gates[mb] - hi.astype(F32)).astype(BF)
+        for k, v in enumerate((route_ids[mb].astype(F32).astype(BF), hi, lo)):
+            at = D + 48 * mb + 16 * k
+            T0[z, yh, c, :, at:at + TOPK] = v
     pl.semaphore_wait(barrier, 7)
 
     sib_count = [0, 0]
@@ -100,29 +106,22 @@
             ref = T[mb].at[0, 0, 0]
             remote(ref, ref, ags_s.at[mb, k], ags_r.at[mb, k], sibling).wait_recv()
 
+    def ring_copy(mb, sgn, d, rel, hop):
+        dr = 0 if sgn > 0 else 1
+        ref = chunk(mb, zat(-sgn * (d + hop)), yh if rel == 0 else 1 - yh)
+        if d == 3:
+            ref = ref.at[pl.ds(dr * (TOK // 2), TOK // 2)]
+        return remote(ref, ref, agr_s.at[mb, dr, d, rel], agr_r.at[mb, dr, d, rel], at_z(sgn))
+
     def ring(mb, sgn, d, rel):
-        dr = 0 if sgn > 0 else 1
-        if d == 3:
-            ys = dr
-        else:
-            ys = yh if rel == 0 else 1 - yh
-        ref = chunk(mb, zat(-sgn * d), ys)
-        go(("ag", mb), remote(ref, ref, agr_s.at[mb, dr, d, rel], agr_r.at[mb, dr, d, rel], at_z(sgn)))
-
-    def ring_wait(mb, sgn, d, rel):
-        dr = 0 if sgn > 0 else 1
-        if d == 4:
-            ys = dr
-        else:
-            ys = yh if rel == 0 else 1 - yh
-        zs = zat(-sgn * d)
+        go(("ag", mb), ring_copy(mb, sgn, d, rel, 0))
+
+    def cross_over(mb, k, zs, ys):
         ref = chunk(mb, zs, ys)
-        remote(ref, ref, agr_s.at[mb, dr, d - 1, rel], agr_r.at[mb, dr, d - 1, rel], at_z(sgn)).wait_recv()
-        to_sibling(mb, zs, ys)
+        return remote(ref, ref, agy_s.at[mb, k], agy_r.at[mb, k], ypart)
 
     def ag_y(mb):
-        ref = chunk(mb, z, yh)
-        go(("ag", mb), remote(ref, ref, agy_s.at[mb], agy_r.at[mb], ypart))
+        go(("ag", mb), cross_over(mb, 0, z, yh))
 
     def ag_own(mb):
         for sgn in (1, -1):
@@ -130,8 +129,7 @@
         to_sibling(mb, z, yh)
 
     def ag_partner(mb):
-        ref = chunk(mb, z, 1 - yh)
-        remote(ref, ref, agy_s.at[mb], agy_r.at[mb], ypart).wait_recv()
+        cross_over(mb, 0, z, 1 - yh).wait_recv()
         for sgn in (1, -1):
             ring(mb, sgn, 0, 1)
         to_sibling(mb, z, 1 - yh)
@@ -139,14 +137,28 @@
     def ag_step(mb, d):
         for rel in (0, 1):
             for sgn in (1, -1):
-                if d == 4 and rel == 1:
+                if rel == 1 and d > PZ:
                     continue
-                ring_wait(mb, sgn, d, rel)
-                if d < 3:
+                zs = zat(-sgn * d)
+                ring_copy(mb, sgn, d - 1, rel, 1).wait_recv()
+                if d < (4 if rel == 0 else PZ):
                     ring(mb, sgn, d, rel)
-        if d == 3:
-            for sgn in (1, -1):
-                ring(mb, sgn, 3, 0)
+                if d < 4:
+                    to_sibling(mb, zs, yh if rel == 0 else 1 - yh)
+                if PZ < d < 4:
+                    go(("ag", mb), cross_over(mb, 1 if sgn > 0 else 2, zs, yh))
+        if d == 4:
+            to_sibling(mb, zat(4), yh)
+            if PZ == 4:
+                to_sibling(mb, zat(4), 1 - yh)
+            else:
+                go(("ag", mb), cross_over(mb, 3, zat(4), yh))
+
+    def ag_land(mb):
+        for k, d in ((1, -3), (2, 3), (3, 4)):
+            if abs(d) > PZ:
+                cross_over(mb, k, zat(d), 1 - yh).wait_recv()
+                to_sibling(mb, zat(d), 1 - yh)
 
     x_first, y_first = [(1, 0)], [(0, 0), (0, 1), (1, 1)]
 
@@ -215,6 +227,13 @@
                 Q0[j, :, 0:512] = WI[1, dp, pl.ds(pl.multiple_of(i * 16, 16), 16), h * 512:(h + 1) * 512]
                 Q0[j, :, 512:768] = WO[1, dp, pl.ds(pl.multiple_of(j * 16, 16), 16), :]
         Q1[ex] = Q0[ex]
+
+        @pl.loop(0, NEX)
+        def _(s):
+            wanted, found = new_plan[s], jnp.int32(0)
+            for r in range(1, NEX):
+                found = jnp.where(plan[r] == wanted, r, found)
+            source[s] = found
 
     def spread(src, dst, ss, rs):
         @pl.loop(1, NEX)
@@ -298,13 +317,12 @@
             up = jnp.dot(xs, WI[s, :, :, pl.ds(col + F, 256)].reshape(D, 256), preferred_element_type=F32)
             H[:, pl.ds(col, 256)] = (gate / (1.0 + jnp.exp(-gate)) * up).astype(BF)
 
-        @pl.loop(0, NDP)
-        def _(b):
+        for b in range(NDP):
             y = jnp.dot(H[...], WO[s, b], preferred_element_type=F32).astype(BF)
-            XY[mb, :, s, :, pl.ds(pl.multiple_of(b * DK, DK), DK)] = y.reshape(NZ, ROWS, DK)
+            XY[mb, :, s, :, b * DK:(b + 1) * DK] = y.reshape(NZ, ROWS, DK)
 
     def part(mb, zd, core, rels, n):
-        cols = pl.ds(pl.multiple_of(n * NB, NB), NB)
+        cols = pl.ds(n * NB, NB)
         if len(rels) == 2:
             g = GT[mb, zd, :, core].reshape(NYH * TOK, 256)
         else:
@@ -332,9 +350,8 @@
         def _(i):
             zd = turn(i)
 
-            @pl.loop(0, D // NB)
-            def _(n):
-                cols = pl.ds(pl.multiple_of(n * NB, NB), NB)
+            for n in range(D // NB):
+                cols = pl.ds(n * NB, NB)
                 v = part(mb, zd, 1 - c, (0, 1), n).astype(BF)
                 for rel in range(2):
                     sref(mb, zd, rel, cols)[...] = v[rel]
@@ -358,7 +375,7 @@
         )
 
     def cross_slot(mb, i):
-        return RV.at[mb, (0, 0, 1)[i], (0, 1, 1)[i], 1]
+        return RV.at[mb, (0, 0, 1, 0, 1)[i], (0, 1, 1, 2, 2)[i], 1]
 
     def cross_copy(mb, i, h, zd):
         return remote(
@@ -372,15 +389,13 @@
     def pre(slot, mb, zd, i, rel):
         sib_copy(mb, i, rel, zd).wait_recv()
 
-        @pl.loop(0, D // NB)
-        def _(n):
-            cols = pl.ds(pl.multiple_of(n * NB, NB), NB)
+        for n in range(D // NB):
+            cols = pl.ds(n * NB, NB)
             PRE[slot, :, cols] = part(mb, zd, c, (rel,), n)[0] + dref(mb, zd, rel, cols)[...].astype(F32)
 
     def put(slot, h, arrived, out):
-        @pl.loop(0, D // NB)
-        def _(n):
-            cols = pl.ds(pl.multiple_of(n * NB, NB), NB)
+        for n in range(D // NB):
+            cols = pl.ds(n * NB, NB)
             acc = PRE[slot, half(h), cols]
             for ref in arrived:
                 acc = acc + ref[half(h), cols].astype(F32)
@@ -393,18 +408,14 @@
             put(0, h, [], dref(mb, zd, 1))
             go("rs", cross_copy(mb, i, h, zd))
 
-    def rs_other(mb, j):
-        at = [(dr, 2 * (4 - j) - 1 + dr, turn(2 * (4 - j) - 1 + dr)) for dr in (0, 1)]
+    def rs_other(mb):
+        at = [(dr, 5 + dr, turn(5 + dr)) for dr in (0, 1)]
         for dr, i, zd in at:
             pre(dr, mb, zd, i, 1)
         for h in (0, 1):
             for dr, i, zd in at:
-                arrived = []
-                if j == 1:
-                    rs_copy(mb, dr, 2, 1, h, zd).wait_recv()
-                    arrived.append(RV.at[mb, dr, 2, 1])
-                put(dr, h, arrived, dref(mb, zd, 1))
-                go("rs", rs_copy(mb, dr, 4 - j, 1, h, zd))
+                put(dr, h, [], dref(mb, zd, 1))
+                go("rs", rs_copy(mb, dr, 3, 1, h, zd))
 
     def rs_far(mb):
         zd = turn(0)
@@ -422,7 +433,7 @@
             for dr, i, zd in at:
                 h = turn_h if dr == 1 else 1 - turn_h
                 arrived = []
-                if j == 3:
+                if j >= 2:
                     cross_copy(mb, i, h, zd).wait_recv()
                     arrived.append(cross_slot(mb, i))
                 if j < 3 or h == dr:
@@ -484,6 +495,7 @@
     for sgn in (1, -1):
         w1x_wait(sgn, 2)
     w1y(3)
+    ag_land(0)
     wait_sibling(0)
     pick(0)
     ag_step(1, 2)
@@ -507,16 +519,18 @@
         to_sib(mb, 1, 3)
         cross(mb, 1)
         cross(mb, 2)
+        to_sib(mb, 5, 7)
+        rs_other(mb)
+        rs_far(mb)
         to_sib(mb, 3, 5)
-        rs_other(mb, 2)
-        rs_far(mb)
+        cross(mb, 3)
+        cross(mb, 4)
 
     def rs_second(mb):
-        to_sib(mb, 5, 7)
-        rs_other(mb, 1)
         rs_own(mb, 3)
 
     rs_first(0)
+    ag_land(1)
     wait_sibling(1)
     pick(1)
     rs_second(0)
@@ -549,26 +563,15 @@
 
 
 def on_device(tokens, route_ids, route_gates, expert_in, expert_out, old_plan, new_plan):
-    source = jnp.argmax(old_plan[None, :] == new_plan[:, None], axis=1).astype(jnp.int32)
-    hi = lax.reduce_precision(route_gates, 8, 7)
-    lo = lax.reduce_precision(route_gates - hi, 8, 7)
-    fill = ((0, 0), (0, 16 - TOPK))
-    parts = []
-    for mb in range(MB):
-        parts.append(jnp.pad(route_ids[mb].astype(F32), fill, constant_values=-1.0))
-        parts.append(jnp.pad(hi[mb], fill))
-        parts.append(jnp.pad(lo[mb], fill))
-    parts.append(jnp.zeros((TOK, 128 - 48 * MB), F32))
-    meta = jnp.concatenate(parts, axis=1).astype(BF)
     dma = pltpu.SemaphoreType.DMA
     hbm = pl.BlockSpec(memory_space=pl.ANY)
     smem = pl.BlockSpec(memory_space=pltpu.SMEM)
     vmem = pl.BlockSpec(memory_space=pltpu.VMEM)
     sems = [
         (8,),
-        (MB, 2, 4, 2), (MB, 2, 4, 2), (MB,), (MB,), (MB, 16), (MB, 16),
+        (MB, 2, 4, 2), (MB, 2, 4, 2), (MB, 4), (MB, 4), (MB, 16), (MB, 16),
         (2, 2, 1), (2, 2, 1), (4, 1), (4, 1), (3,), (3,), (2, 2, 2, 3), (2, 2, 2, 3),
-        (MB, NZ, 2), (MB, NZ, 2), (MB, 2, 4, 2, 2), (MB, 2, 4, 2, 2), (MB, 2), (MB, 2), (MB, 3, 2), (MB, 3, 2),
+        (MB, NZ, 2), (MB, NZ, 2), (MB, 2, 4, 2, 2), (MB, 2, 4, 2, 2), (MB, 2), (MB, 2), (MB, 5, 2), (MB, 5, 2),
         (NEX,), (NEX,), (NEX,), (NEX,),
     ]
     return pl.pallas_call(
@@ -578,7 +581,7 @@
             jax.ShapeDtypeStruct((1, DK, 2 * F), BF),
             jax.ShapeDtypeStruct((1, F, DK), BF),
         ),
-        in_specs=[hbm, hbm, hbm, hbm, smem, smem],
+        in_specs=[hbm, vmem, vmem, hbm, hbm, smem, smem],
         out_specs=(vmem, vmem, vmem),
         scratch_shapes=[
             pltpu.VMEM((NZ, NYH, NC, TOK, WIDE), BF),
@@ -598,6 +601,7 @@
             pltpu.VMEM((NEX, 16, 768), BF),
             pltpu.VMEM((NEX, 16, 768), BF),
             pltpu.VMEM((NEX, 16, 768), BF),
+            pltpu.SMEM((NEX,), jnp.int32),
         ]
         + [dma(shape) for shape in sems],
         compiler_params=pltpu.CompilerParams(
@@ -606,7 +610,7 @@
         cost_estimate=pl.CostEstimate(
             flops=MB * 12 * 2**30, bytes_accessed=4 * 2**20, transcendentals=MB * 768 * F
         ),
-    )(tokens, meta, expert_in, expert_out, old_plan, source)
+    )(tokens, route_ids, route_gates, expert_in, expert_out, old_plan, new_plan)
 
 
 def solution(mesh):

time: 226 us -> 211 us (0.934)
  Pallas kernels: 217 us -> 204 us
    pallas_call x1, Pallas kernels: 217 us -> 204 us  [on_device(): pl.pallas_call(kernel, out_shape=(jax.ShapeDtypeStruct((MB, TOK, D), BF),...]
    unnamed x12 -> x11, local copies, waits for them, and re-layouts: 4.7 us -> 5.9 us
where the time goes in v3:
time: 211 us
  Pallas kernels  204 us (97%)
  local copies, waits for them, and re-layouts  5.9 us (3%)
    pallas_call x1, Pallas kernels, on_device(): pl.pallas_call(kernel, out_shape=(jax.ShapeDtypeStruct((MB, TOK, D), BF),...  204 us
    unnamed x11, local copies, waits for them, and re-layouts  5.9 us

profile of v3, /device:TPU:1, one launch (start us, length us, event | category | flops | bytes accessed | tf_op | source)
XLA Modules:
  0.0 210.6 jit_solution(3210914822436556951)
XLA Ops:
  0.6 0.0 copy-start.2
  0.6 1.4 copy.10.route_ids
  2.1 0.0 copy-done.2
  2.1 0.7 copy.11.route_gates
  2.8 204.0 %shard_map.94 = (bf16[2,64,2048]{2,1,0:T(8,128)(2,1)}, bf16[1,256,1024]{2,1,0:T(8,128)(2,1)}, bf16[1,512,256]{2,1,0:T(8,128)(2,1)}) custom-call(bf16[2,64,2048]{2,1,0:T(8,128)(2,1)} %tokens.1, s32[2,64,10]{2,1,0:T(8,128)} %copy.10.route_ids, f32[2,64,10]{2,1,0:T(8,128)} %copy.11.route_gates, bf16[1,2,256,1024]{3,2,1,0:T(8,128)(2,1)} %expert_in.1, ...), custom_call_target="tpu_custom_call" | custom-call | flops 25769803776 | bytes 4194304 | tf_op jit(solution)/shard_map/pallas_call | solution.py:577
  206.8 0.0 copy-start
  206.8 1.9 copy.15
  208.8 0.0 copy-done
  208.8 0.0 copy-start.1
  208.8 0.8 copy.16
  209.6 0.3 copy-done.1
  209.9 0.7 copy.17
Async XLA Ops:
  0.6 1.4 copy-start.2
  206.8 2.0 copy-start
  208.8 1.1 copy-start.1

commit v4 on v3

--- a/solution.py
+++ b/solution.py
@@ -464,12 +464,12 @@
     ag_own(0)
     for cp in loads_w:
         cp.wait()
+    w0y()
     for sgn in (1, -1):
         w1x(sgn, 0)
-    w0y()
-    w1y(0)
     for sgn in (1, -1):
         w0x(sgn, 0, 0)
+    w1y(0)
     for cp in loads_t[1]:
         cp.wait()
     ag_y(1)
@@ -508,9 +508,9 @@
     for rel in (0, 1):
         for sgn in (1, -1):
             w0x_wait(sgn, 2, rel)
+    ffn(0, 0)
     for k in range(4):
         w1y_wait(k)
-    ffn(0, 0)
     ffn(0, 1)
     drain(("ag", 0))
     def rs_first(mb):
@@ -539,9 +539,9 @@
     spread(Q2, Q3, q2_s, q2_r)
     ffn(1, 0)
     ffn(1, 1)
-    rs_own(0, 2)
     drain(("ag", 1))
     rs_first(1)
+    rs_own(0, 2)
     to_sib(0, 7, 8)
     rs_own(0, 1)
     rs_second(1)

time: 211 us -> 211 us (level); the launches traced: 211 us -> 208 us
    pallas_call x1, Pallas kernels: 204 us -> 202 us  [on_device(): pl.pallas_call(kernel, out_shape=(jax.ShapeDtypeStruct((MB, TOK, D), BF),...]
where the time goes in v4:
time: 211 us; the launch traced here: 208 us
  Pallas kernels  202 us (96%)
  local copies, waits for them, and re-layouts  5.9 us (3%)
    pallas_call x1, Pallas kernels, on_device(): pl.pallas_call(kernel, out_shape=(jax.ShapeDtypeStruct((MB, TOK, D), BF),...  202 us
    unnamed x11, local copies, waits for them, and re-layouts  5.9 us

profile of v4, /device:TPU:1, one launch (start us, length us, event | category | flops | bytes accessed | tf_op | source)
XLA Modules:
  0.0 208.3 jit_solution(13194628840871260903)
XLA Ops:
  0.6 0.0 copy-start.2
  0.6 1.4 copy.10.route_ids
  2.1 0.0 copy-done.2
  2.1 0.7 copy.11.route_gates
  2.8 201.8 %shard_map.94 = (bf16[2,64,2048]{2,1,0:T(8,128)(2,1)}, bf16[1,256,1024]{2,1,0:T(8,128)(2,1)}, bf16[1,512,256]{2,1,0:T(8,128)(2,1)}) custom-call(bf16[2,64,2048]{2,1,0:T(8,128)(2,1)} %tokens.1, s32[2,64,10]{2,1,0:T(8,128)} %copy.10.route_ids, f32[2,64,10]{2,1,0:T(8,128)} %copy.11.route_gates, bf16[1,2,256,1024]{3,2,1,0:T(8,128)(2,1)} %expert_in.1, ...), custom_call_target="tpu_custom_call" | custom-call | flops 25769803776 | bytes 4194304 | tf_op jit(solution)/shard_map/pallas_call | solution.py:577
  204.6 0.0 copy-start
  204.6 1.9 copy.15
  206.5 0.0 copy-done
  206.5 0.0 copy-start.1
  206.5 0.8 copy.16
  207.3 0.3 copy-done.1
  207.6 0.7 copy.17
Async XLA Ops:
  0.6 1.4 copy-start.2
  204.6 2.0 copy-start
  206.5 1.1 copy-start.1
